TPU v7x, 32 devices: a whole 2x2x4 slice. The times are simulated.
32 devices in a mesh: dp: 2 (over x), row: 4 (over z), col: 4 (over y, core).
Axes of the slice: x: 2, y: 2, z: 4, core: 2. Of those that a mesh axis runs over, the one named last changes fastest.
Arguments:
- tokens: bfloat16 [4, 4096, 1024], P(None, ('dp', 'row', 'col')), may hold values from -6 to 6
- lengths: int32 [2, 4], P('dp'), may hold values from 512 to 2048, as said below
- first_gain: float32 [1024], replicated, may hold values from 0.5 to 1.5
- first_shift: float32 [1024], replicated, may hold values from -1.25 to 1.25
- w_query: bfloat16 [1024, 1024], P(('dp', 'row'), 'col'), may hold values from -0.1875 to 0.1875
- w_key: bfloat16 [1024, 1024], P(('dp', 'row'), 'col'), may hold values from -0.1875 to 0.1875
- w_value: bfloat16 [1024, 1024], P(('dp', 'row'), 'col'), may hold values from -0.1875 to 0.1875
- bias_query: float32 [1024], P('col'), may hold values from -3 to 3
- bias_value: float32 [1024], P('col'), may hold values from -0.3125 to 0.3125
- w_output: bfloat16 [1024, 1024], P('col', ('dp', 'row')), may hold values from -2 to 2
- bias_output: float32 [1024], replicated, may hold values from -1.25 to 1.25
- second_gain: float32 [1024], replicated, may hold values from 0.5 to 1.5
- second_shift: float32 [1024], replicated, may hold values from -1.25 to 1.25
- w_up: bfloat16 [1024, 4096], P(('dp', 'row'), 'col'), may hold values from -0.1875 to 0.1875
- bias_up: float32 [4096], P('col'), may hold values from -1.75 to 1.75
- w_down: bfloat16 [4096, 1024], P('col', ('dp', 'row')), may hold values from -0.09375 to 0.09375
- bias_down: float32 [1024], replicated, may hold values from -1.25 to 1.25
- cotangent: bfloat16 [4, 4096, 1024], P(None, ('dp', 'row', 'col')), may hold values from -6 to 6
Outputs:
- output: bfloat16 [4, 4096, 1024], P(None, ('dp', 'row', 'col'))
- grad_tokens: bfloat16 [4, 4096, 1024], P(None, ('dp', 'row', 'col'))
- grad_first_gain: float32 [1024], replicated
- grad_first_shift: float32 [1024], replicated
- grad_w_query: float32 [1024, 1024], P(('dp', 'row'), 'col')
- grad_w_key: float32 [1024, 1024], P(('dp', 'row'), 'col')
- grad_w_value: float32 [1024, 1024], P(('dp', 'row'), 'col')
- grad_bias_query: float32 [1024], P('col')
- grad_bias_value: float32 [1024], P('col')
- grad_w_output: float32 [1024, 1024], P('col', ('dp', 'row'))
- grad_bias_output: float32 [1024], replicated
- grad_second_gain: float32 [1024], replicated
- grad_second_shift: float32 [1024], replicated
- grad_w_up: float32 [1024, 4096], P(('dp', 'row'), 'col')
- grad_bias_up: float32 [4096], P('col')
- grad_w_down: float32 [4096, 1024], P('col', ('dp', 'row'))
- grad_bias_down: float32 [1024], replicated
Inputs may be any that keep to these rules, and one draw needn't show every extreme that they name: `lengths`: in every group one of the 4 sequences, which one drawn from the seed, has exactly 2048 valid tokens.
All inputs are finite; a program needn't handle non-finite values.
Results may differ from a plain program's by a relative error of at most 0.012.
Values may be sent and summed in bfloat16 or wider, within the bound.
A program may use at most 192 MiB of HBM per device.

v0:
```python
import jax
import jax.numpy as jnp
from jax import lax
from jax.sharding import PartitionSpec as P

HD = 64


EPSILON = 1e-05
MASKED = -1e30


def layer_norm(values, norm_gain, norm_shift):
    centered = values - jnp.mean(values, axis=-1, keepdims=True)
    variance = jnp.mean(centered * centered, axis=-1, keepdims=True)
    return centered * lax.rsqrt(variance + EPSILON) * norm_gain + norm_shift


def gelu_tanh(values):
    return jax.nn.gelu(values, approximate=True)


def product(former, latter):
    return jnp.dot(former, latter, preferred_element_type=jnp.float32)


def transposed_left(former, latter):
    return lax.dot_general(
        former, latter, (((0,), (0,)), ((), ())), preferred_element_type=jnp.float32
    )


def transposed_right(former, latter):
    return lax.dot_general(
        former, latter, (((1,), (1,)), ((), ())), preferred_element_type=jnp.float32
    )


def spread_rows(rows_block):
    return lax.all_gather(rows_block, "col", axis=0, tiled=True)


def fold_rows(partial_sum):
    return lax.psum_scatter(partial_sum, "col", scatter_dimension=0, tiled=True)


def fetch_weights(w_query, w_key, w_value, w_up, w_output, w_down):
    leading = (
        lax.all_gather(w_query, ("dp", "row"), axis=0, tiled=True),
        lax.all_gather(w_key, ("dp", "row"), axis=0, tiled=True),
        lax.all_gather(w_value, ("dp", "row"), axis=0, tiled=True),
        lax.all_gather(w_up, ("dp", "row"), axis=0, tiled=True),
    )
    trailing = (
        lax.all_gather(w_output, ("dp", "row"), axis=1, tiled=True),
        lax.all_gather(w_down, ("dp", "row"), axis=1, tiled=True),
    )
    return tuple(leading) + tuple(trailing)


def reduce_blocks(gradients):
    leading = (
        lax.psum_scatter(gradients[0], ("dp", "row"), scatter_dimension=0, tiled=True),
        lax.psum_scatter(gradients[1], ("dp", "row"), scatter_dimension=0, tiled=True),
        lax.psum_scatter(gradients[2], ("dp", "row"), scatter_dimension=0, tiled=True),
        lax.psum_scatter(gradients[3], ("dp", "row"), scatter_dimension=0, tiled=True),
    )
    trailing = (
        lax.psum_scatter(gradients[4], ("dp", "row"), scatter_dimension=1, tiled=True),
        lax.psum_scatter(gradients[5], ("dp", "row"), scatter_dimension=1, tiled=True),
    )
    return tuple(leading) + tuple(trailing)


def heads_of(rows_block):
    return rows_block.reshape(rows_block.shape[0], -1, HD)


def block_of(rows_all, start, block_rows):
    return heads_of(lax.dynamic_slice_in_dim(rows_all, start, block_rows, 0))


def block_scores(query_heads, key_heads, query_start, key_start, length):
    block_rows = query_heads.shape[0]
    scores = jnp.einsum(
        "qhd,khd->hqk", query_heads, key_heads, preferred_element_type=jnp.float32
    ) * HD ** (-0.5)
    query_pos = query_start + jnp.arange(block_rows, dtype=jnp.int32)
    key_pos = key_start + jnp.arange(key_heads.shape[0], dtype=jnp.int32)
    allowed = (key_pos[None, :] <= query_pos[:, None]) & (key_pos[None, :] < length)
    return jnp.where(allowed[None], scores, MASKED)


def key_block_count(row_place, length, block_rows):
    return jnp.minimum(row_place + 1, (length + block_rows - 1) // block_rows)


def attention_forward(queries, key_rows, value_rows, row_place, length):
    block_rows = queries.shape[0]
    query_heads = heads_of(queries)
    head_count = query_heads.shape[1]
    query_start = row_place * block_rows
    count = key_block_count(row_place, length, block_rows)

    def stats_step(block_index, carry):
        highest, partition = carry
        start = block_index * block_rows
        scores = block_scores(
            query_heads, block_of(key_rows, start, block_rows), query_start, start, length
        )
        newest = jnp.maximum(highest, jnp.max(scores, axis=-1, keepdims=True))
        partition = partition * jnp.exp(highest - newest) + jnp.sum(
            jnp.exp(scores - newest), axis=-1, keepdims=True
        )
        return (newest, partition)

    start_stats = (
        jnp.full((head_count, block_rows, 1), MASKED, jnp.float32),
        jnp.zeros((head_count, block_rows, 1), jnp.float32),
    )
    highest, partition = lax.fori_loop(0, count, stats_step, start_stats)

    def output_step(block_index, total):
        start = block_index * block_rows
        scores = block_scores(
            query_heads, block_of(key_rows, start, block_rows), query_start, start, length
        )
        weights_low = (jnp.exp(scores - highest) / partition).astype(jnp.bfloat16)
        return total + jnp.einsum(
            "hqk,khd->qhd",
            weights_low,
            block_of(value_rows, start, block_rows),
            preferred_element_type=jnp.float32,
        )

    total = lax.fori_loop(0, count, output_step, jnp.zeros(query_heads.shape, jnp.float32))
    return (total.reshape(block_rows, -1), highest, partition)


def attention_query_side(
    queries, key_rows, value_rows, grad_attended, highest, partition, row_place, length
):
    block_rows = queries.shape[0]
    seq_rows = key_rows.shape[0]
    query_heads = heads_of(queries)
    grad_heads = heads_of(grad_attended)
    head_count = query_heads.shape[1]
    query_start = row_place * block_rows
    count = key_block_count(row_place, length, block_rows)

    def inner_step(block_index, total):
        start = block_index * block_rows
        scores = block_scores(
            query_heads, block_of(key_rows, start, block_rows), query_start, start, length
        )
        weights = jnp.exp(scores - highest) / partition
        grad_weights = jnp.einsum(
            "qhd,khd->hqk",
            grad_heads,
            block_of(value_rows, start, block_rows),
            preferred_element_type=jnp.float32,
        )
        return total + jnp.sum(weights * grad_weights, axis=-1, keepdims=True)

    inner = lax.fori_loop(0, count, inner_step, jnp.zeros((head_count, block_rows, 1), jnp.float32))

    def grad_step(block_index, carry):
        start = block_index * block_rows
        key_heads = block_of(key_rows, start, block_rows)
        scores = block_scores(query_heads, key_heads, query_start, start, length)
        weights = jnp.exp(scores - highest) / partition
        grad_weights = jnp.einsum(
            "qhd,khd->hqk",
            grad_heads,
            block_of(value_rows, start, block_rows),
            preferred_element_type=jnp.float32,
        )
        grad_scores = (weights * (grad_weights - inner)).astype(jnp.bfloat16)
        query_total = carry[0] + jnp.einsum(
            "hqk,khd->qhd", grad_scores, key_heads, preferred_element_type=jnp.float32
        )
        weights_low = weights.astype(jnp.bfloat16)
        key_part = jnp.einsum(
            "hqk,qhd->khd", grad_scores, query_heads, preferred_element_type=jnp.float32
        )
        value_part = jnp.einsum(
            "hqk,qhd->khd", weights_low, grad_heads, preferred_element_type=jnp.float32
        )
        key_total = lax.dynamic_update_slice_in_dim(
            carry[1], lax.dynamic_slice_in_dim(carry[1], start, block_rows, 0) + key_part, start, 0
        )
        value_total = lax.dynamic_update_slice_in_dim(
            carry[2],
            lax.dynamic_slice_in_dim(carry[2], start, block_rows, 0) + value_part,
            start,
            0,
        )
        return (query_total, key_total, value_total)

    start_carry = (jnp.zeros(query_heads.shape, jnp.float32),)
    start_carry = start_carry + (
        jnp.zeros((seq_rows, head_count, HD), jnp.float32),
        jnp.zeros((seq_rows, head_count, HD), jnp.float32),
    )
    totals = lax.fori_loop(0, count, grad_step, start_carry)
    query_terms = totals[0].reshape(block_rows, -1) * HD ** (-0.5)
    return (
        query_terms,
        totals[1].reshape(seq_rows, -1) * HD ** (-0.5),
        totals[2].reshape(seq_rows, -1),
        inner,
    )


def local(
    tokens,
    lengths,
    first_gain,
    first_shift,
    w_query,
    w_key,
    w_value,
    bias_query,
    bias_value,
    w_output,
    bias_output,
    second_gain,
    second_shift,
    w_up,
    bias_up,
    w_down,
    bias_down,
    cotangent,
):
    micro_count, own_rows, width = tokens.shape
    col_count = lax.axis_size("col")
    group_rows = own_rows * col_count
    row_place = lax.axis_index("row")
    col_place = lax.axis_index("col")
    head_width = w_query.shape[1]
    hidden_width = w_up.shape[1]
    own_positions = (
        row_place * group_rows + col_place * own_rows + jnp.arange(own_rows, dtype=jnp.int32)
    )
    weight_totals = (
        jnp.zeros((width, head_width), jnp.float32),
        jnp.zeros((width, head_width), jnp.float32),
        jnp.zeros((width, head_width), jnp.float32),
        jnp.zeros((width, hidden_width), jnp.float32),
        jnp.zeros((head_width, width), jnp.float32),
        jnp.zeros((hidden_width, width), jnp.float32),
    )
    vector_totals = (
        jnp.zeros((width,), jnp.float32),
        jnp.zeros((width,), jnp.float32),
        jnp.zeros((head_width,), jnp.float32),
        jnp.zeros((head_width,), jnp.float32),
        jnp.zeros((width,), jnp.float32),
        jnp.zeros((width,), jnp.float32),
        jnp.zeros((width,), jnp.float32),
        jnp.zeros((hidden_width,), jnp.float32),
        jnp.zeros((width,), jnp.float32),
    )
    results = []
    input_grads = []
    for micro_index in range(micro_count):
        gathered = fetch_weights(w_query, w_key, w_value, w_up, w_output, w_down)
        query_full, key_full, value_full, up_full, output_full, down_full = gathered
        length = lengths[0, micro_index]
        inputs = tokens[micro_index].astype(jnp.float32)
        normed = layer_norm(inputs, first_gain, first_shift).astype(jnp.bfloat16)
        normed_all = spread_rows(normed)
        queries = (product(normed_all, query_full) + bias_query).astype(jnp.bfloat16)
        keys_local = product(normed_all, key_full).astype(jnp.bfloat16)
        values_local = (product(normed_all, value_full) + bias_value).astype(jnp.bfloat16)
        keys_all, values_all = (
            lax.all_gather(keys_local, "row", axis=0, tiled=True),
            lax.all_gather(values_local, "row", axis=0, tiled=True),
        )
        attended, maxima, partitions = attention_forward(
            queries, keys_all, values_all, row_place, length
        )
        attended_low = attended.astype(jnp.bfloat16)
        branch = fold_rows(product(attended_low, output_full)) + bias_output
        middle = inputs + branch
        second_normed = layer_norm(middle, second_gain, second_shift).astype(jnp.bfloat16)
        second_all = spread_rows(second_normed)
        pre_activation = product(second_all, up_full) + bias_up
        activated = gelu_tanh(pre_activation).astype(jnp.bfloat16)
        result = middle + (fold_rows(product(activated, down_full)) + bias_down)
        results.append(result.astype(jnp.bfloat16))
        query_full, key_full, value_full, up_full, output_full, down_full = fetch_weights(
            w_query, w_key, w_value, w_up, w_output, w_down
        )
        validity = (own_positions < length).astype(jnp.float32)
        grad_result = cotangent[micro_index].astype(jnp.float32) * validity[:, None]
        grad_result_all = spread_rows(grad_result.astype(jnp.bfloat16))
        grad_down = transposed_left(activated, grad_result_all)
        grad_activated = transposed_right(grad_result_all, down_full)
        gelu_back = jax.vjp(gelu_tanh, pre_activation)[1]
        grad_pre = gelu_back(grad_activated)[0].astype(jnp.bfloat16)
        grad_up = transposed_left(second_all, grad_pre)
        grad_second_normed = fold_rows(transposed_right(grad_pre, up_full))
        second_back = jax.vjp(layer_norm, middle, second_gain, second_shift)[1]
        grad_middle_norm, grad_second_gain, grad_second_shift = second_back(grad_second_normed)
        grad_middle = grad_result + grad_middle_norm
        grad_branch = grad_middle.astype(jnp.bfloat16)
        grad_branch_all = spread_rows(grad_branch)
        grad_output = transposed_left(attended_low, grad_branch_all)
        grad_attended = transposed_right(grad_branch_all, output_full).astype(jnp.bfloat16)
        query_terms, key_terms, value_terms, inner = attention_query_side(
            queries, keys_all, values_all, grad_attended, maxima, partitions, row_place, length
        )
        key_sums, value_sums = (
            lax.psum_scatter(key_terms, "row", scatter_dimension=0, tiled=True),
            lax.psum_scatter(value_terms, "row", scatter_dimension=0, tiled=True),
        )
        grad_queries = query_terms.astype(jnp.bfloat16)
        grad_keys = key_sums.astype(jnp.bfloat16)
        grad_values = value_sums.astype(jnp.bfloat16)
        grad_query = transposed_left(normed_all, grad_queries)
        grad_key = transposed_left(normed_all, grad_keys)
        grad_value = transposed_left(normed_all, grad_values)
        grad_normed = fold_rows(
            transposed_right(grad_queries, query_full)
            + transposed_right(grad_keys, key_full)
            + transposed_right(grad_values, value_full)
        )
        first_back = jax.vjp(layer_norm, inputs, first_gain, first_shift)[1]
        grad_inputs_norm, grad_first_gain, grad_first_shift = first_back(grad_normed)
        input_grads.append((grad_middle + grad_inputs_norm).astype(jnp.bfloat16))
        local_grads = (grad_query, grad_key, grad_value, grad_up, grad_output, grad_down)
        weight_totals = tuple(
            (former + latter for former, latter in zip(weight_totals, local_grads))
        )
        local_vectors = (
            grad_first_gain,
            grad_first_shift,
            jnp.sum(grad_queries.astype(jnp.float32), axis=0),
            jnp.sum(grad_values.astype(jnp.float32), axis=0),
            jnp.sum(grad_branch.astype(jnp.float32), axis=0),
            grad_second_gain,
            grad_second_shift,
            jnp.sum(grad_pre.astype(jnp.float32), axis=0),
            jnp.sum(grad_result, axis=0),
        )
        vector_totals = tuple(
            (former + latter for former, latter in zip(vector_totals, local_vectors))
        )
    weight_totals = reduce_blocks(weight_totals)

    def widen(vector_part):
        blank = jnp.zeros((vector_part.shape[0] * col_count,), jnp.float32)
        return lax.dynamic_update_slice(blank, vector_part, (col_place * vector_part.shape[0],))

    def narrow(whole_vector, piece_width):
        return lax.dynamic_slice_in_dim(whole_vector, col_place * piece_width, piece_width)

    (
        sum_first_gain,
        sum_first_shift,
        sum_bias_query,
        sum_bias_value,
        sum_bias_output,
        sum_second_gain,
        sum_second_shift,
        sum_bias_up,
        sum_bias_down,
    ) = lax.psum(
        (
            vector_totals[0],
            vector_totals[1],
            widen(vector_totals[2]),
            widen(vector_totals[3]),
            vector_totals[4],
            vector_totals[5],
            vector_totals[6],
            widen(vector_totals[7]),
            vector_totals[8],
        ),
        ("dp", "row", "col"),
    )
    grad_w_query, grad_w_key, grad_w_value, grad_w_up, grad_w_output, grad_w_down = weight_totals
    return (
        jnp.stack(results, axis=0),
        jnp.stack(input_grads, axis=0),
        sum_first_gain,
        sum_first_shift,
        grad_w_query,
        grad_w_key,
        grad_w_value,
        narrow(sum_bias_query, head_width),
        narrow(sum_bias_value, head_width),
        grad_w_output,
        sum_bias_output,
        sum_second_gain,
        sum_second_shift,
        grad_w_up,
        narrow(sum_bias_up, hidden_width),
        grad_w_down,
        sum_bias_down,
    )


def solution(mesh):
    return jax.shard_map(
        local,
        mesh=mesh,
        in_specs=(
            P(None, ("dp", "row", "col"), None),
            P("dp", None),
            P(),
            P(),
            P(("dp", "row"), "col"),
            P(("dp", "row"), "col"),
            P(("dp", "row"), "col"),
            P("col"),
            P("col"),
            P("col", ("dp", "row")),
            P(),
            P(),
            P(),
            P(("dp", "row"), "col"),
            P("col"),
            P("col", ("dp", "row")),
            P(),
            P(None, ("dp", "row", "col"), None),
        ),
        out_specs=(
            P(None, ("dp", "row", "col"), None),
            P(None, ("dp", "row", "col"), None),
            P(),
            P(),
            P(("dp", "row"), "col"),
            P(("dp", "row"), "col"),
            P(("dp", "row"), "col"),
            P("col"),
            P("col"),
            P("col", ("dp", "row")),
            P(),
            P(),
            P(),
            P(("dp", "row"), "col"),
            P("col"),
            P("col", ("dp", "row")),
            P(),
        ),
        check_vma=False,
    )
```

profile of v0, /device:TPU:0, one launch (start us, length us, event | category | flops | bytes accessed | tf_op | source)
XLA Modules:
  0.0 2150.5 jit_solution(12603748127288404223)
XLA Ops:
  14.9 34.1 %all_gather.63 = bf16[1024,256]{1,0:T(8,128)(2,1)S(1)} all-gather(bf16[128,256]{1,0:T(8,128)(2,1)S(1)} %copy-done.104), channel_id=1, replica_groups=mesh['dp'=2,'row'=4,'col'=4] {'dp','row'}, dimensions={0}, use_global_device_ids=true | all-gather | bytes 589824 | tf_op jit(solution)/shard_map/all_gather | solution.py:50
  51.7 32.6 %all_gather.61 = bf16[1024,256]{1,0:T(8,128)(2,1)S(1)} all-gather(bf16[128,256]{1,0:T(8,128)(2,1)S(1)} %copy-done.105), channel_id=1, replica_groups=mesh['dp'=2,'row'=4,'col'=4] {'dp','row'}, dimensions={0}, use_global_device_ids=true | all-gather | bytes 589824 | tf_op jit(solution)/shard_map/all_gather | solution.py:51
  95.6 35.5 %all_gather.65 = bf16[1024,256]{1,0:T(8,128)(2,1)S(1)} all-gather(bf16[128,256]{1,0:T(8,128)(2,1)S(1)} %copy-done.106), channel_id=1, replica_groups=mesh['dp'=2,'row'=4,'col'=4] {'dp','row'}, dimensions={0}, use_global_device_ids=true | all-gather | bytes 589824 | tf_op jit(solution)/shard_map/all_gather | solution.py:49
  131.1 32.6 %all_gather.66 = bf16[256,1024]{1,0:T(8,128)(2,1)} all-gather(bf16[256,128]{1,0:T(8,128)(2,1)S(1)} %copy-done.107), channel_id=1, replica_groups=mesh['dp'=2,'row'=4,'col'=4] {'dp','row'}, dimensions={1}, use_global_device_ids=true | all-gather | bytes 589824 | tf_op jit(solution)/shard_map/all_gather | solution.py:55
  216.0 13.3 all-gather.43.cloned.1.call-done
  233.8 24.6 %all-gather.41.cloned.1.call-done = bf16[2048,256]{1,0:T(8,128)(2,1)} async-done(((bf16[512,256]{1,0:T(8,128)(2,1)}), bf16[2048,256]{1,0:T(8,128)(2,1)}) %all-gather.41.cloned.1.call-update) | async-done | bytes 1048592 | tf_op jit(solution)/shard_map/all_gather | solution.py:278
  277.5 14.2 reduce-scatter.43.cloned.1.call-done
  291.7 34.1 %reduce-scatter.39.cloned.1.call-done = f32[128,1024]{1,0:T(8,128)} async-done(((f32[512,1024]{1,0:T(8,128)}), f32[128,1024]{1,0:T(8,128)}) %reduce-scatter.39.cloned.1.call-update) | async-done | bytes 524304 | tf_op jit(solution)/shard_map/reduce_scatter | solution.py:44
  325.9 33.9 %reduce-scatter.35.cloned.1.call-done = f32[128,1024]{1,0:T(8,128)} async-done(((f32[512,1024]{1,0:T(8,128)}), f32[128,1024]{1,0:T(8,128)}) %reduce-scatter.35.cloned.1.call-update) | async-done | bytes 524304 | tf_op jit(solution)/shard_map/reduce_scatter | solution.py:44
  365.7 12.4 all-gather.67.cloned.1.call-done
  378.1 53.2 %all-gather.37.cloned.1.call-done = bf16[1024,1024]{1,0:T(8,128)(2,1)} async-done(((bf16[1024,128]{1,0:T(8,128)(2,1)}), bf16[1024,1024]{1,0:T(8,128)(2,1)}) %all-gather.37.cloned.1.call-update) | async-done | bytes 2097168 | tf_op jit(solution)/shard_map/all_gather | solution.py:56
  452.2 47.0 %all-gather.35.cloned.1.call-done = bf16[1024,1024]{1,0:T(8,128)(2,1)} async-done(((bf16[128,1024]{1,0:T(8,128)(2,1)}), bf16[1024,1024]{1,0:T(8,128)(2,1)}) %all-gather.35.cloned.1.call-update) | async-done | bytes 2097168 | tf_op jit(solution)/shard_map/all_gather | solution.py:52
  499.2 17.3 all-gather.45.cloned.1.call-done
  521.0 13.8 all-gather.53.cloned.1.call-done
  539.3 13.9 all-gather.61.cloned.1.call-done
  557.7 13.8 all-gather.71.cloned.1.call-done
  618.9 32.1 %reduce-scatter.55.cloned.1.call-done = f32[128,1024]{1,0:T(8,128)} async-done(((f32[512,1024]{1,0:T(8,128)}), f32[128,1024]{1,0:T(8,128)}) %reduce-scatter.55.cloned.1.call-update) | async-done | bytes 524304 | tf_op jit(solution)/shard_map/reduce_scatter | solution.py:44
  651.0 34.2 %reduce-scatter.63.cloned.1.call-done = f32[128,1024]{1,0:T(8,128)} async-done(((f32[512,1024]{1,0:T(8,128)}), f32[128,1024]{1,0:T(8,128)}) %reduce-scatter.63.cloned.1.call-update) | async-done | bytes 524304 | tf_op jit(solution)/shard_map/reduce_scatter | solution.py:44
  685.1 33.8 %reduce-scatter.45.cloned.1.call-done = f32[128,1024]{1,0:T(8,128)} async-done(((f32[512,1024]{1,0:T(8,128)}), f32[128,1024]{1,0:T(8,128)}) %reduce-scatter.45.cloned.1.call-update) | async-done | bytes 524304 | tf_op jit(solution)/shard_map/reduce_scatter | solution.py:44
  722.6 30.6 %reduce-scatter.37.cloned.1.call-done = f32[128,1024]{1,0:T(8,128)} async-done(((f32[512,1024]{1,0:T(8,128)}), f32[128,1024]{1,0:T(8,128)}) %reduce-scatter.37.cloned.1.call-update) | async-done | bytes 524304 | tf_op jit(solution)/shard_map/reduce_scatter | solution.py:44
  753.2 33.8 %reduce-scatter.41.cloned.1.call-done = f32[128,1024]{1,0:T(8,128)} async-done(((f32[512,1024]{1,0:T(8,128)}), f32[128,1024]{1,0:T(8,128)}) %reduce-scatter.41.cloned.1.call-update) | async-done | bytes 524304 | tf_op jit(solution)/shard_map/reduce_scatter | solution.py:44
  793.7 15.3 all-gather.73.cloned.1.call-done
  881.5 37.7 %reduce-scatter.65.cloned.1.call-done = f32[512,256]{0,1:T(8,128)} async-done(((f32[2048,256]{0,1:T(8,128)}), f32[512,256]{0,1:T(8,128)}) %reduce-scatter.65.cloned.1.call-update) | async-done | bytes 524304 | tf_op jit(solution)/shard_map/reduce_scatter | solution.py:315
  922.1 42.5 %reduce-scatter.67.cloned.1.call-done = f32[512,256]{0,1:T(8,128)} async-done(((f32[2048,256]{0,1:T(8,128)}), f32[512,256]{0,1:T(8,128)}) %reduce-scatter.67.cloned.1.call-update) | async-done | bytes 524304 | tf_op jit(solution)/shard_map/reduce_scatter | solution.py:316
  972.0 38.2 %reduce-scatter.73.cloned.1.call-done = f32[512,256]{0,1:T(8,128)} async-done(((f32[2048,256]{0,1:T(8,128)}), f32[512,256]{0,1:T(8,128)}) %reduce-scatter.73.cloned.1.call-update) | async-done | bytes 524304 | tf_op jit(solution)/shard_map/reduce_scatter | solution.py:315
  1013.1 42.5 %reduce-scatter.75.cloned.1.call-done = f32[512,256]{0,1:T(8,128)} async-done(((f32[2048,256]{0,1:T(8,128)}), f32[512,256]{0,1:T(8,128)}) %reduce-scatter.75.cloned.1.call-update) | async-done | bytes 524304 | tf_op jit(solution)/shard_map/reduce_scatter | solution.py:316
  1062.4 38.8 %reduce-scatter.57.cloned.1.call-done = f32[512,256]{0,1:T(8,128)} async-done(((f32[2048,256]{0,1:T(8,128)}), f32[512,256]{0,1:T(8,128)}) %reduce-scatter.57.cloned.1.call-update) | async-done | bytes 524304 | tf_op jit(solution)/shard_map/reduce_scatter | solution.py:315
  1104.1 42.6 %reduce-scatter.59.cloned.1.call-done = f32[512,256]{0,1:T(8,128)} async-done(((f32[2048,256]{0,1:T(8,128)}), f32[512,256]{0,1:T(8,128)}) %reduce-scatter.59.cloned.1.call-update) | async-done | bytes 524304 | tf_op jit(solution)/shard_map/reduce_scatter | solution.py:316
  1151.6 28.4 %reduce-scatter.69.cloned.1.call-done = f32[128,1024]{1,0:T(8,128)} async-done(((f32[512,1024]{1,0:T(8,128)}), f32[128,1024]{1,0:T(8,128)}) %reduce-scatter.69.cloned.1.call-update) | async-done | bytes 524304 | tf_op jit(solution)/shard_map/reduce_scatter | solution.py:44
  1180.1 33.8 %reduce-scatter.77.cloned.1.call-done = f32[128,1024]{1,0:T(8,128)} async-done(((f32[512,1024]{1,0:T(8,128)}), f32[128,1024]{1,0:T(8,128)}) %reduce-scatter.77.cloned.1.call-update) | async-done | bytes 524304 | tf_op jit(solution)/shard_map/reduce_scatter | solution.py:44
  1213.9 34.2 %reduce-scatter.61.cloned.1.call-done = f32[128,1024]{1,0:T(8,128)} async-done(((f32[512,1024]{1,0:T(8,128)}), f32[128,1024]{1,0:T(8,128)}) %reduce-scatter.61.cloned.1.call-update) | async-done | bytes 524304 | tf_op jit(solution)/shard_map/reduce_scatter | solution.py:44
  1251.8 16.6 all-gather.27.cloned.1.call-done
  1276.8 22.1 %all-gather.31.cloned.1.call-done = bf16[2048,256]{1,0:T(8,128)(2,1)} async-done(((bf16[512,256]{1,0:T(8,128)(2,1)}), bf16[2048,256]{1,0:T(8,128)(2,1)}) %all-gather.31.cloned.1.call-update) | async-done | bytes 1048592 | tf_op jit(solution)/shard_map/all_gather | solution.py:277
  1303.3 25.2 %all-gather.29.cloned.1.call-done = bf16[2048,256]{1,0:T(8,128)(2,1)} async-done(((bf16[512,256]{1,0:T(8,128)(2,1)}), bf16[2048,256]{1,0:T(8,128)(2,1)}) %all-gather.29.cloned.1.call-update) | async-done | bytes 1048592 | tf_op jit(solution)/shard_map/all_gather | solution.py:278
  1341.3 43.3 %reduce-scatter.31.cloned.1.call-done = f32[128,1024]{1,0:T(8,128)} async-done(((f32[512,1024]{1,0:T(8,128)}), f32[128,1024]{1,0:T(8,128)}) %reduce-scatter.31.cloned.1.call-update) | async-done | bytes 524304 | tf_op jit(solution)/shard_map/reduce_scatter | solution.py:44
  1387.6 16.1 all-gather.33.cloned.1.call-done
  1408.3 13.9 all-gather.63.cloned.1.call-done
  1435.9 26.2 %reduce-scatter.47.cloned.1.call-done = f32[128,1024]{1,0:T(8,128)} async-done(((f32[512,1024]{1,0:T(8,128)}), f32[128,1024]{1,0:T(8,128)}) %reduce-scatter.47.cloned.1.call-update) | async-done | bytes 524304 | tf_op jit(solution)/shard_map/reduce_scatter | solution.py:44
  1463.5 32.5 %reduce-scatter.33.cloned.1.call-done = f32[128,1024]{1,0:T(8,128)} async-done(((f32[512,1024]{1,0:T(8,128)}), f32[128,1024]{1,0:T(8,128)}) %reduce-scatter.33.cloned.1.call-update) | async-done | bytes 524304 | tf_op jit(solution)/shard_map/reduce_scatter | solution.py:44
  1500.2 16.8 all-gather.65.cloned.1.call-done
  1541.4 69.6 %reduce-scatter.49.cloned.1.call-done = f32[512,256]{0,1:T(8,128)} async-done(((f32[2048,256]{0,1:T(8,128)}), f32[512,256]{0,1:T(8,128)}) %reduce-scatter.49.cloned.1.call-update) | async-done | bytes 524304 | tf_op jit(solution)/shard_map/reduce_scatter | solution.py:315
  1613.8 42.5 %reduce-scatter.51.cloned.1.call-done = f32[512,256]{0,1:T(8,128)} async-done(((f32[2048,256]{0,1:T(8,128)}), f32[512,256]{0,1:T(8,128)}) %reduce-scatter.51.cloned.1.call-update) | async-done | bytes 524304 | tf_op jit(solution)/shard_map/reduce_scatter | solution.py:316
  1716.0 40.8 %all-reduce = (f32[1024]{0:T(1024)}, f32[1024]{0:T(1024)}, f32[1024]{0:T(1024)S(1)}, f32[1024]{0:T(1024)S(1)}, f32[1024]{0:T(1024)}, /*index=5*/f32[1024]{0:T(10...) all-reduce(f32[1024]{0:T(1024)S(1)} %add_add_fusion.19, ...), channel_id=1, replica_groups=mesh['dp'=2,'row'=4,'col'=4] {'dp','row','col'}, use_global_device_ids=true, to_apply=%region_104.105 | all-reduce | flops 12288 | bytes 98304 | tf_op jit(solution)/shard_map/psum | solution.py:369
  1763.7 61.8 %reduce-scatter.79.cloned.1.call-done = f32[128,256]{1,0:T(8,128)} async-done(((f32[1024,256]{1,0:T(8,128)}), f32[128,256]{1,0:T(8,128)}) %reduce-scatter.79.cloned.1.call-update) | async-done | bytes 131088 | tf_op jit(solution)/shard_map/reduce_scatter | solution.py:63
  1825.5 91.6 %reduce-scatter.89.cloned.1.call-done = f32[1024,128]{1,0:T(8,128)} async-done(((f32[1024,1024]{1,0:T(8,128)}), f32[1024,128]{1,0:T(8,128)}) %reduce-scatter.89.cloned.1.call-update) | async-done | bytes 524304 | tf_op jit(solution)/shard_map/reduce_scatter | solution.py:70
  1917.1 92.3 %reduce-scatter.87.cloned.1.call-done = f32[128,1024]{1,0:T(8,128)} async-done(((f32[1024,1024]{1,0:T(8,128)}), f32[128,1024]{1,0:T(8,128)}) %reduce-scatter.87.cloned.1.call-update) | async-done | bytes 524304 | tf_op jit(solution)/shard_map/reduce_scatter | solution.py:66
  2009.4 67.2 %reduce-scatter.83.cloned.1.call-done = f32[128,256]{1,0:T(8,128)} async-done(((f32[1024,256]{1,0:T(8,128)}), f32[128,256]{1,0:T(8,128)}) %reduce-scatter.83.cloned.1.call-update) | async-done | bytes 131088 | tf_op jit(solution)/shard_map/reduce_scatter | solution.py:65
  2076.6 66.9 %reduce-scatter.81.cloned.1.call-done = f32[128,256]{1,0:T(8,128)} async-done(((f32[1024,256]{1,0:T(8,128)}), f32[128,256]{1,0:T(8,128)}) %reduce-scatter.81.cloned.1.call-update) | async-done | bytes 131088 | tf_op jit(solution)/shard_map/reduce_scatter | solution.py:64
  (862 shorter events, 528.8 us)
Async XLA Ops:
  13.4 72.2 %all-gather.47.cloned.1.call-start = ((), (), s32[]{:S(2)}) async-start(), calls=%async_computation.44 | async-start | bytes 1310720 | tf_op jit(solution)/shard_map/all_gather | solution.py:40
  14.2 76.4 %all-gather.39.cloned.1.call-start = ((), (), s32[]{:S(2)}) async-start(), calls=%async_computation.38 | async-start | bytes 1310720 | tf_op jit(solution)/shard_map/all_gather | solution.py:40
  14.9 156.0 %all-gather.59.cloned.1.call-start = ((), (), s32[]{:S(2)}) async-start(), calls=%async_computation.52 | async-start | bytes 1310720 | tf_op jit(solution)/shard_map/all_gather | solution.py:277
  51.7 123.6 %all-gather.57.cloned.1.call-start = ((), (), s32[]{:S(2)}) async-start(), calls=%async_computation.51 | async-start | bytes 1310720 | tf_op jit(solution)/shard_map/all_gather | solution.py:278
  85.5 98.8 %all-gather.51.cloned.1.call-start = ((), (), s32[]{:S(2)}) async-start(), calls=%async_computation.46 | async-start | bytes 1310720 | tf_op jit(solution)/shard_map/all_gather | solution.py:277
  88.0 112.3 %all-gather.49.cloned.1.call-start = ((), (), s32[]{:S(2)}) async-start(), calls=%async_computation.45 | async-start | bytes 1310720 | tf_op jit(solution)/shard_map/all_gather | solution.py:278
  90.5 138.9 %all-gather.43.cloned.1.call-start = ((), (), s32[]{:S(2)}) async-start(), calls=%async_computation.40 | async-start | bytes 1310720 | tf_op jit(solution)/shard_map/all_gather | solution.py:277
  93.0 165.4 %all-gather.41.cloned.1.call-start = ((), (), s32[]{:S(2)}) async-start(), calls=%async_computation.39 | async-start | bytes 1310720 | tf_op jit(solution)/shard_map/all_gather | solution.py:278
  170.8 120.9 %reduce-scatter.43.cloned.1.call-start = ((), (), s32[]{:S(2)}) async-start(), calls=%async_computation.53 | async-start | bytes 2621440 | tf_op jit(solution)/shard_map/reduce_scatter | solution.py:44
  216.0 109.9 %reduce-scatter.39.cloned.1.call-start = ((), (), s32[]{:S(2)}) async-start(), calls=%async_computation.47 | async-start | bytes 2621440 | tf_op jit(solution)/shard_map/reduce_scatter | solution.py:44
  233.7 126.0 %reduce-scatter.35.cloned.1.call-start = ((), (), s32[]{:S(2)}) async-start(), calls=%async_computation.41 | async-start | bytes 2621440 | tf_op jit(solution)/shard_map/reduce_scatter | solution.py:44
  271.5 106.7 %all-gather.67.cloned.1.call-start = ((), (), s32[]{:S(2)}) async-start(), calls=%async_computation.62 | async-start | bytes 1310720 | tf_op jit(solution)/shard_map/all_gather | solution.py:40
  275.7 155.6 %all-gather.37.cloned.1.call-start = ((), (), s32[]{:S(2)}) async-start(), calls=%async_computation.36 | async-start | bytes 2359296 | tf_op jit(solution)/shard_map/all_gather | solution.py:56
  276.3 171.4 %all-gather.75.cloned.1.call-start = ((), (), s32[]{:S(2)}) async-start(), calls=%async_computation.74 | async-start | bytes 1310720 | tf_op jit(solution)/shard_map/all_gather | solution.py:40
  276.9 222.4 %all-gather.35.cloned.1.call-start = ((), (), s32[]{:S(2)}) async-start(), calls=%async_computation.35 | async-start | bytes 2359296 | tf_op jit(solution)/shard_map/all_gather | solution.py:52
  277.5 239.1 %all-gather.45.cloned.1.call-start = ((), (), s32[]{:S(2)}) async-start(), calls=%async_computation.42 | async-start | bytes 1310720 | tf_op jit(solution)/shard_map/all_gather | solution.py:40
  363.4 171.4 %all-gather.53.cloned.1.call-start = ((), (), s32[]{:S(2)}) async-start(), calls=%async_computation.48 | async-start | bytes 1310720 | tf_op jit(solution)/shard_map/all_gather | solution.py:40
  363.9 189.3 %all-gather.61.cloned.1.call-start = ((), (), s32[]{:S(2)}) async-start(), calls=%async_computation.54 | async-start | bytes 1310720 | tf_op jit(solution)/shard_map/all_gather | solution.py:40
  364.7 206.8 %all-gather.71.cloned.1.call-start = ((), (), s32[]{:S(2)}) async-start(), calls=%async_computation.68 | async-start | bytes 1310720 | tf_op jit(solution)/shard_map/all_gather | solution.py:40
  365.3 251.7 %reduce-scatter.71.cloned.1.call-start = ((), (), s32[]{:S(2)}) async-start(), calls=%async_computation.75 | async-start | bytes 2621440 | tf_op jit(solution)/shard_map/reduce_scatter | solution.py:44
  585.4 65.6 %reduce-scatter.55.cloned.1.call-start = ((), (), s32[]{:S(2)}) async-start(), calls=%async_computation.63 | async-start | bytes 2621440 | tf_op jit(solution)/shard_map/reduce_scatter | solution.py:44
  590.8 94.3 %reduce-scatter.63.cloned.1.call-start = ((), (), s32[]{:S(2)}) async-start(), calls=%async_computation.69 | async-start | bytes 2621440 | tf_op jit(solution)/shard_map/reduce_scatter | solution.py:44
  596.6 122.4 %reduce-scatter.45.cloned.1.call-start = ((), (), s32[]{:S(2)}) async-start(), calls=%async_computation.55 | async-start | bytes 2621440 | tf_op jit(solution)/shard_map/reduce_scatter | solution.py:44
  601.9 151.3 %reduce-scatter.37.cloned.1.call-start = ((), (), s32[]{:S(2)}) async-start(), calls=%async_computation.43 | async-start | bytes 2621440 | tf_op jit(solution)/shard_map/reduce_scatter | solution.py:44
  607.3 179.7 %reduce-scatter.41.cloned.1.call-start = ((), (), s32[]{:S(2)}) async-start(), calls=%async_computation.49 | async-start | bytes 2621440 | tf_op jit(solution)/shard_map/reduce_scatter | solution.py:44
  612.5 196.6 %all-gather.73.cloned.1.call-start = ((), (), s32[]{:S(2)}) async-start(), calls=%async_computation.70 | async-start | bytes 1310720 | tf_op jit(solution)/shard_map/all_gather | solution.py:40
  793.7 125.5 %reduce-scatter.65.cloned.1.call-start = ((), (), s32[]{:S(2)}) async-start(), calls=%async_computation.71 | async-start | bytes 2621440 | tf_op jit(solution)/shard_map/reduce_scatter | solution.py:315
  832.6 132.0 %reduce-scatter.67.cloned.1.call-start = ((), (), s32[]{:S(2)}) async-start(), calls=%async_computation.72 | async-start | bytes 2621440 | tf_op jit(solution)/shard_map/reduce_scatter | solution.py:316
  838.0 172.3 %reduce-scatter.73.cloned.1.call-start = ((), (), s32[]{:S(2)}) async-start(), calls=%async_computation.77 | async-start | bytes 2621440 | tf_op jit(solution)/shard_map/reduce_scatter | solution.py:315
  853.3 202.3 %reduce-scatter.75.cloned.1.call-start = ((), (), s32[]{:S(2)}) async-start(), calls=%async_computation.78 | async-start | bytes 2621440 | tf_op jit(solution)/shard_map/reduce_scatter | solution.py:316
  860.8 240.4 %reduce-scatter.57.cloned.1.call-start = ((), (), s32[]{:S(2)}) async-start(), calls=%async_computation.65 | async-start | bytes 2621440 | tf_op jit(solution)/shard_map/reduce_scatter | solution.py:315
  877.2 269.5 %reduce-scatter.59.cloned.1.call-start = ((), (), s32[]{:S(2)}) async-start(), calls=%async_computation.66 | async-start | bytes 2621440 | tf_op jit(solution)/shard_map/reduce_scatter | solution.py:316
  878.0 302.1 %reduce-scatter.69.cloned.1.call-start = ((), (), s32[]{:S(2)}) async-start(), calls=%async_computation.73 | async-start | bytes 2621440 | tf_op jit(solution)/shard_map/reduce_scatter | solution.py:44
  968.8 245.1 %reduce-scatter.77.cloned.1.call-start = ((), (), s32[]{:S(2)}) async-start(), calls=%async_computation.79 | async-start | bytes 2621440 | tf_op jit(solution)/shard_map/reduce_scatter | solution.py:44
  1059.8 188.2 %reduce-scatter.61.cloned.1.call-start = ((), (), s32[]{:S(2)}) async-start(), calls=%async_computation.67 | async-start | bytes 2621440 | tf_op jit(solution)/shard_map/reduce_scatter | solution.py:44
  1151.0 117.4 %all-gather.27.cloned.1.call-start = ((), (), s32[]{:S(2)}) async-start(), calls=%async_computation.30 | async-start | bytes 1310720 | tf_op jit(solution)/shard_map/all_gather | solution.py:40
  1276.8 107.8 %reduce-scatter.31.cloned.1.call-start = ((), (), s32[]{:S(2)}) async-start(), calls=%async_computation.33 | async-start | bytes 2621440 | tf_op jit(solution)/shard_map/reduce_scatter | solution.py:44
  1387.6 74.5 %reduce-scatter.47.cloned.1.call-start = ((), (), s32[]{:S(2)}) async-start(), calls=%async_computation.57 | async-start | bytes 2621440 | tf_op jit(solution)/shard_map/reduce_scatter | solution.py:44
  1435.9 81.1 %all-gather.65.cloned.1.call-start = ((), (), s32[]{:S(2)}) async-start(), calls=%async_computation.58 | async-start | bytes 1310720 | tf_op jit(solution)/shard_map/all_gather | solution.py:40
  1500.1 110.8 %reduce-scatter.49.cloned.1.call-start = ((), (), s32[]{:S(2)}) async-start(), calls=%async_computation.59 | async-start | bytes 2621440 | tf_op jit(solution)/shard_map/reduce_scatter | solution.py:315
  1539.4 116.9 %reduce-scatter.51.cloned.1.call-start = ((), (), s32[]{:S(2)}) async-start(), calls=%async_computation.60 | async-start | bytes 2621440 | tf_op jit(solution)/shard_map/reduce_scatter | solution.py:316
  1540.0 171.0 %reduce-scatter.53.cloned.1.call-start = ((), (), s32[]{:S(2)}) async-start(), calls=%async_computation.61 | async-start | bytes 2621440 | tf_op jit(solution)/shard_map/reduce_scatter | solution.py:44
  1659.9 103.7 %reduce-scatter.85.cloned.1.call-start = ((), (), s32[]{:S(2)}) async-start(), calls=%async_computation.83 | async-start | bytes 1179648 | tf_op jit(solution)/shard_map/reduce_scatter | solution.py:69
  1665.7 159.8 %reduce-scatter.79.cloned.1.call-start = ((), (), s32[]{:S(2)}) async-start(), calls=%async_computation.80 | async-start | bytes 1179648 | tf_op jit(solution)/shard_map/reduce_scatter | solution.py:63
  1671.3 245.8 %reduce-scatter.89.cloned.1.call-start = ((), (), s32[]{:S(2)}) async-start(), calls=%async_computation.85 | async-start | bytes 4718592 | tf_op jit(solution)/shard_map/reduce_scatter | solution.py:70
  1683.2 326.2 %reduce-scatter.87.cloned.1.call-start = ((), (), s32[]{:S(2)}) async-start(), calls=%async_computation.84 | async-start | bytes 4718592 | tf_op jit(solution)/shard_map/reduce_scatter | solution.py:66
  1693.3 383.4 %reduce-scatter.83.cloned.1.call-start = ((), (), s32[]{:S(2)}) async-start(), calls=%async_computation.82 | async-start | bytes 1179648 | tf_op jit(solution)/shard_map/reduce_scatter | solution.py:65
  1702.4 441.2 %reduce-scatter.81.cloned.1.call-start = ((), (), s32[]{:S(2)}) async-start(), calls=%async_computation.81 | async-start | bytes 1179648 | tf_op jit(solution)/shard_map/reduce_scatter | solution.py:64
  (202 other events, 5675.5 us)
Sparse Core Ops, SparseCore 0:
  13.5 19.4 all-gather.54
  72.2 31.8 all-gather.58
  106.1 35.5 all-gather.56
  143.2 28.1 all-gather.50
  173.0 27.3 all-gather.48
  201.9 27.4 all-gather.42
  230.9 27.4 all-gather.40
  260.8 30.9 reduce-scatter.42
  294.4 31.3 reduce-scatter.38
  328.3 31.4 reduce-scatter.34
  380.2 51.0 all-gather.36
  449.9 49.2 all-gather.34
  536.4 16.7 all-gather.60
  554.7 16.7 all-gather.70
  585.5 31.4 reduce-scatter.70
  619.5 31.4 reduce-scatter.54
  653.7 31.4 reduce-scatter.62
  687.5 31.4 reduce-scatter.44
  721.7 31.4 reduce-scatter.36
  755.5 31.4 reduce-scatter.40
  792.3 16.7 all-gather.72
  810.7 16.7 all-gather.76
  829.6 16.7 all-gather.68
  848.7 70.4 reduce-scatter.64
  921.5 43.0 reduce-scatter.66
  967.0 43.1 reduce-scatter.72
  1012.4 43.1 reduce-scatter.74
  1058.0 43.1 reduce-scatter.56
  1103.5 43.1 reduce-scatter.58
  1149.3 30.7 reduce-scatter.68
  1182.4 31.4 reduce-scatter.76
  1216.6 31.4 reduce-scatter.60
  1270.9 27.9 all-gather.30
  1301.1 27.4 all-gather.28
  1341.3 43.1 reduce-scatter.30
  1387.0 16.7 all-gather.32
  1430.7 31.4 reduce-scatter.46
  1464.5 31.4 reduce-scatter.32
  1500.2 16.7 all-gather.64
  1539.5 71.3 reduce-scatter.48
  1613.1 43.1 reduce-scatter.50
  1660.0 30.7 reduce-scatter.52
  1694.7 63.9 reduce-scatter.84
  1763.0 62.4 reduce-scatter.78
  1829.6 87.4 reduce-scatter.88
  1921.7 87.6 reduce-scatter.86
  2013.4 63.1 reduce-scatter.82
  2081.0 62.4 reduce-scatter.80
  (8 shorter events, 130.0 us)
where the time goes:
time: 2180 us; the launch traced here: 2150 us
  waiting for transfers between devices  1550 us (71%)
  matrix products  245 us (11%)
  blocking collectives  176 us (8%)
  other arithmetic  89.1 us (4%)
  local copies, waits for them, and re-layouts  64.4 us (3%)
    reduce_scatter x16, waiting for transfers between devices, fold_rows(): return lax.psum_scatter(partial_sum, 'col', scatter_dimension=0, tiled=True)  449 us
    reduce_scatter x4, waiting for transfers between devices, local(): lax.psum_scatter(key_terms, 'row', scatter_dimension=0, tiled=True)  184 us
    reduce_scatter x4, waiting for transfers between devices, local(): lax.psum_scatter(value_terms, 'row', scatter_dimension=0, tiled=True)  170 us
    all_gather x16, waiting for transfers between devices, spread_rows(): return lax.all_gather(rows_block, 'col', axis=0, tiled=True)  162 us
    reduce_scatter x1, waiting for transfers between devices, reduce_blocks(): lax.psum_scatter(gradients[3], ('dp', 'row'), scatter_dimension=0, tiled=...  92.3 us
    reduce_scatter x1, waiting for transfers between devices, reduce_blocks(): lax.psum_scatter(gradients[5], ('dp', 'row'), scatter_dimension=1, tiled=...  91.6 us
    dot_general x24, matrix products, transposed_right(): lax.dot_general(former, latter, (((1,), (1,)), ((), ())), preferred_eleme...  80.8 us
    dot_general x24, matrix products, product(): return jnp.dot(former, latter, preferred_element_type=jnp.float32)  69 us
  transfers between devices with their start and end apart: 56, of which 46 were waited for; matrix products, arithmetic and copies ran while one was open for 14% of the time, Pallas kernels for 0%

commit v1 on v0

--- a/solution.py
+++ b/solution.py
@@ -1,6 +1,10 @@
+import functools
+
 import jax
 import jax.numpy as jnp
 from jax import lax
+from jax.experimental import pallas as pl
+from jax.experimental.pallas import tpu as pltpu
 from jax.sharding import PartitionSpec as P
 
 HD = 64
@@ -212,7 +216,7 @@
     )
 
 
-def local(
+def local_general(
     tokens,
     lengths,
     first_gain,
@@ -402,9 +406,337 @@
     )
 
 
+F32 = jnp.float32
+LOW = jnp.bfloat16
+VMEM_LIMIT = 56 * 1024 * 1024
+
+
+def fits(mesh):
+    return mesh.shape["row"] == 4 and mesh.shape["col"] == 4 and mesh.shape["dp"] == 2
+
+
+def contract(former, latter, former_dim, latter_dim):
+    return lax.dot_general(
+        former,
+        latter,
+        (((former_dim,), (latter_dim,)), ((), ())),
+        preferred_element_type=jnp.float32,
+    )
+
+
+def attention_out_kernel(q_ref, k_ref, v_ref, key_bias_ref, causal_ref, o_ref, lse_ref):
+    block = q_ref.shape[0]
+    chunks = k_ref.shape[0] // block
+    place = pl.program_id(1)
+    lane = lax.broadcasted_iota(jnp.int32, q_ref.shape, 1)
+    queries = q_ref[...]
+    for index in range(chunks):
+
+        @pl.when(place == index)
+        def _():
+            wide = (index + 1) * block
+            parts = []
+            for head in range(2):
+                mine = (lane // HD) == head
+                masked = jnp.where(mine, queries, 0) * jnp.asarray(HD**-0.5, LOW)
+                scores = contract(masked, k_ref[:wide], 1, 1) + key_bias_ref[:, :wide]
+                last = scores[:, wide - block :] + causal_ref[...]
+                scores = last if index == 0 else jnp.concatenate([scores[:, : wide - block], last], axis=1)
+                highest = jnp.max(scores, axis=1, keepdims=True)
+                weights = jnp.exp(scores - highest)
+                total = jnp.sum(weights, axis=1, keepdims=True)
+                parts.append(contract(weights.astype(LOW), v_ref[:wide], 1, 0) / total)
+                spread = jnp.broadcast_to(highest + jnp.log(total), (block, 128))
+                lse_ref[0, 0, head : head + 1, :] = spread.T[:1]
+            o_ref[...] = jnp.where(lane < HD, parts[0], parts[1]).astype(LOW)
+
+
+def attention_out(queries, keys, values, key_bias, causal):
+    rows, width = queries.shape
+    block = causal.shape[0]
+    pairs, chunks = width // 128, rows // block
+    row_spec = pl.BlockSpec((block, 128), lambda p, r: (r, p))
+    full_spec = pl.BlockSpec((rows, 128), lambda p, r: (0, p))
+    return pl.pallas_call(
+        attention_out_kernel,
+        grid=(pairs, chunks),
+        in_specs=[
+            row_spec,
+            full_spec,
+            full_spec,
+            pl.BlockSpec((1, rows), lambda p, r: (0, 0)),
+            pl.BlockSpec((block, block), lambda p, r: (0, 0)),
+        ],
+        out_specs=[row_spec, pl.BlockSpec((1, 1, 2, block), lambda p, r: (p, r, 0, 0))],
+        out_shape=[
+            jax.ShapeDtypeStruct((rows, width), LOW),
+            jax.ShapeDtypeStruct((pairs, chunks, 2, block), F32),
+        ],
+        compiler_params=pltpu.CompilerParams(vmem_limit_bytes=VMEM_LIMIT),
+        cost_estimate=pl.CostEstimate(flops=40_000_000_000, bytes_accessed=4_000_000, transcendentals=0),
+        name="attention_out",
+    )(queries, keys, values, key_bias.reshape(1, rows), causal)
+
+
+def attention_back_kernel(
+    q_ref, k_ref, v_ref, do_ref, o_ref, lse_ref, key_bias_ref, causal_ref, dq_ref, dk_ref, dv_ref, dk_sum, dv_sum
+):
+    block = q_ref.shape[0]
+    chunks = k_ref.shape[0] // block
+    place = pl.program_id(1)
+    lane = lax.broadcasted_iota(jnp.int32, q_ref.shape, 1)
+    queries = q_ref[...]
+    grads = do_ref[...]
+    inner = (grads.astype(F32) * o_ref[...].astype(F32)).T
+
+    @pl.when(place == 0)
+    def _():
+        dk_sum[...] = jnp.zeros_like(dk_sum)
+        dv_sum[...] = jnp.zeros_like(dv_sum)
+
+    for index in range(chunks):
+
+        @pl.when(place == index)
+        def _():
+            wide = (index + 1) * block
+            parts = []
+            for head in range(2):
+                mine = (lane // HD) == head
+                masked = jnp.where(mine, queries, 0) * jnp.asarray(HD**-0.5, LOW)
+                masked_grads = jnp.where(mine, grads, 0)
+                inner_row = jnp.sum(inner[head * HD : (head + 1) * HD], axis=0, keepdims=True)
+                scores = contract(k_ref[:wide], masked, 1, 1) + key_bias_ref[:wide]
+                last = scores[wide - block :] + causal_ref[...]
+                scores = last if index == 0 else jnp.concatenate([scores[: wide - block], last], axis=0)
+                weights = jnp.exp(scores - lse_ref[0, 0, head : head + 1, :])
+                grad_weights = contract(v_ref[:wide], masked_grads, 1, 1)
+                grad_scores = (weights * (grad_weights - inner_row)).astype(LOW)
+                dv_sum[:wide] += contract(weights.astype(LOW), masked_grads, 1, 0)
+                dk_sum[:wide] += contract(grad_scores, masked, 1, 0)
+                parts.append(contract(grad_scores, k_ref[:wide], 0, 0))
+            dq_ref[...] = (jnp.where(lane < HD, parts[0], parts[1]) * HD**-0.5).astype(LOW)
+
+    @pl.when(place == chunks - 1)
+    def _():
+        dk_ref[...] = dk_sum[...].astype(LOW)
+        dv_ref[...] = dv_sum[...].astype(LOW)
+
+
+def attention_back(queries, keys, values, grads, attended, lse, key_bias, causal):
+    rows, width = queries.shape
+    block = causal.shape[0]
+    pairs, chunks = width // 128, rows // block
+    row_spec = pl.BlockSpec((block, 128), lambda p, r: (r, p))
+    full_spec = pl.BlockSpec((rows, 128), lambda p, r: (0, p))
+    return pl.pallas_call(
+        attention_back_kernel,
+        grid=(pairs, chunks),
+        in_specs=[
+            row_spec,
+            full_spec,
+            full_spec,
+            row_spec,
+            row_spec,
+            pl.BlockSpec((1, 1, 2, block), lambda p, r: (p, r, 0, 0)),
+            pl.BlockSpec((rows, 1), lambda p, r: (0, 0)),
+            pl.BlockSpec((block, block), lambda p, r: (0, 0)),
+        ],
+        out_specs=[row_spec, full_spec, full_spec],
+        out_shape=[jax.ShapeDtypeStruct((rows, width), LOW)] * 3,
+        scratch_shapes=[pltpu.VMEM((rows, 128), F32)] * 2,
+        compiler_params=pltpu.CompilerParams(vmem_limit_bytes=VMEM_LIMIT),
+        cost_estimate=pl.CostEstimate(flops=80_000_000_000, bytes_accessed=6_000_000, transcendentals=0),
+        name="attention_back",
+    )(queries, keys, values, grads, attended, lse, key_bias.reshape(rows, 1), causal.T)
+
+
+def swap(array, axis, flip):
+    size = lax.axis_size(axis)
+    return lax.ppermute(array, axis, [(place, place ^ flip) for place in range(size)])
+
+
+def gather_rows(own):
+    core = swap(own, "col", 1)
+    far = swap(own, "col", 2)
+    return jnp.stack([own, core, far, swap(far, "col", 1)], axis=1)
+
+
+def scatter_rows(partial_sum):
+    arrived = swap(partial_sum[:, 1::2], "col", 1)
+    kept = partial_sum[:, 0::2] + arrived
+    return kept[:, 0] + swap(kept[:, 1].astype(LOW), "col", 2).astype(F32)
+
+
+def trade_rows(array):
+    return lax.all_to_all(array, "row", split_axis=0, concat_axis=0)
+
+
+def scatter_blocks(gradient, dim):
+    dp_place = lax.axis_index("dp")
+    row_place = lax.axis_index("row")
+    total = gradient
+    for axis, flip, place in (("dp", 1, dp_place), ("row", 2, row_place // 2), ("row", 1, row_place % 2)):
+        half = total.shape[dim] // 2
+        mine = lax.dynamic_slice_in_dim(total, place * half, half, dim)
+        other = lax.dynamic_slice_in_dim(total, (1 - place) * half, half, dim)
+        total = mine + swap(other.astype(LOW), axis, flip).astype(F32)
+    return total
+
+
+def norm_parts(values):
+    centered = values - jnp.mean(values, axis=-1, keepdims=True)
+    scale = lax.rsqrt(jnp.mean(centered * centered, axis=-1, keepdims=True) + EPSILON)
+    return centered * scale, scale
+
+
+def norm_back(grads, gain, unit, scale):
+    inner = grads * gain
+    mean_inner = jnp.mean(inner, axis=-1, keepdims=True)
+    mean_unit = jnp.mean(inner * unit, axis=-1, keepdims=True)
+    return scale * (inner - mean_inner - unit * mean_unit)
+
+
+def local_sequence(
+    tokens,
+    lengths,
+    first_gain,
+    first_shift,
+    w_query,
+    w_key,
+    w_value,
+    bias_query,
+    bias_value,
+    w_output,
+    bias_output,
+    second_gain,
+    second_shift,
+    w_up,
+    bias_up,
+    w_down,
+    bias_down,
+    cotangent,
+):
+    micro_count, own_rows, width = tokens.shape
+    col_count = lax.axis_size("col")
+    row_place = lax.axis_index("row")
+    col_place = lax.axis_index("col")
+    chunk = own_rows * col_count
+    seq_rows = chunk * micro_count
+    head_width = w_query.shape[1]
+    hidden_width = w_up.shape[1]
+    length = lax.dynamic_slice_in_dim(lengths[0], row_place, 1)[0]
+
+    inside = (col_place ^ jnp.arange(col_count, dtype=jnp.int32))[:, None] * own_rows + jnp.arange(
+        own_rows, dtype=jnp.int32
+    )
+    inside = inside.reshape(-1)
+    positions = (jnp.arange(micro_count, dtype=jnp.int32)[:, None] * chunk + inside).reshape(-1)
+    key_bias = jnp.where(positions < length, 0.0, MASKED).astype(F32)
+    causal = jnp.where(inside[None, :] <= inside[:, None], 0.0, MASKED).astype(F32)
+    own_positions = positions.reshape(micro_count, col_count, own_rows)[:, 0]
+    validity = (own_positions < length).astype(F32)[:, :, None]
+
+    query_key_value = lax.all_gather(
+        jnp.concatenate([w_query, w_key, w_value], axis=1), ("dp", "row"), axis=0, tiled=True
+    )
+    trailing = lax.all_gather(jnp.concatenate([w_output, w_down], axis=0), ("dp", "row"), axis=1, tiled=True)
+    output_full, down_full = trailing[:head_width], trailing[head_width:]
+    up_full = lax.all_gather(w_up, ("dp", "row"), axis=0, tiled=True)
+
+    inputs_low = trade_rows(tokens)
+    inputs = inputs_low.astype(F32)
+    grad_result = trade_rows(cotangent).astype(F32) * validity
+    tokens_all = gather_rows(inputs_low).reshape(seq_rows, width).astype(F32)
+    grad_result_all = gather_rows(grad_result.astype(LOW)).reshape(seq_rows, width)
+
+    normed_all = (norm_parts(tokens_all)[0] * first_gain + first_shift).astype(LOW)
+    projected = product(normed_all, query_key_value)
+    queries = (projected[:, :head_width] + bias_query).astype(LOW)
+    keys = projected[:, head_width : 2 * head_width].astype(LOW)
+    values = (projected[:, 2 * head_width :] + bias_value).astype(LOW)
+    attended, lse = attention_out(queries, keys, values, key_bias, causal)
+
+    def split_rows(array):
+        return array.reshape(micro_count, col_count, own_rows, -1)
+
+    branch = scatter_rows(split_rows(product(attended, output_full))) + bias_output
+    middle = inputs + branch
+    unit, scale = norm_parts(middle)
+    second_normed = (unit * second_gain + second_shift).astype(LOW)
+    second_all = gather_rows(second_normed).reshape(seq_rows, width)
+    pre_activation = product(second_all, up_full) + bias_up
+    activated = gelu_tanh(pre_activation).astype(LOW)
+    result = middle + scatter_rows(split_rows(product(activated, down_full))) + bias_down
+    result = trade_rows(result.astype(LOW))
+
+    grad_down = transposed_left(activated, grad_result_all)
+    grad_activated = transposed_right(grad_result_all, down_full)
+    gelu_back = jax.vjp(gelu_tanh, pre_activation)[1]
+    grad_pre = gelu_back(grad_activated)[0].astype(LOW)
+    grad_up = transposed_left(second_all, grad_pre)
+    grad_second = scatter_rows(split_rows(transposed_right(grad_pre, up_full)))
+    grad_middle = grad_result + norm_back(grad_second, second_gain, unit, scale)
+    grad_branch = grad_middle.astype(LOW)
+    grad_branch_all = gather_rows(grad_branch).reshape(seq_rows, width)
+    grad_output = transposed_left(attended, grad_branch_all)
+    grad_attended = transposed_right(grad_branch_all, output_full).astype(LOW)
+    grad_queries, grad_keys, grad_values = attention_back(
+        queries, keys, values, grad_attended, attended, lse, key_bias, causal
+    )
+    grad_projected = jnp.concatenate([grad_queries, grad_keys, grad_values], axis=1)
+    grad_w = transposed_left(normed_all, grad_projected)
+    grad_first = scatter_rows(split_rows(transposed_right(grad_projected, query_key_value)))
+    first_unit, first_scale = norm_parts(inputs)
+    grad_tokens = grad_middle + norm_back(grad_first, first_gain, first_unit, first_scale)
+    grad_tokens = trade_rows(grad_tokens.astype(LOW))
+
+    grad_w = scatter_blocks(grad_w, 0)
+    grad_trailing = scatter_blocks(jnp.concatenate([grad_output, grad_down], axis=0), 1)
+    grad_up = scatter_blocks(grad_up, 0)
+
+    def over_rows(array):
+        return jnp.sum(array.astype(F32).reshape(-1, array.shape[-1]), axis=0)
+
+    shared = lax.psum(
+        jnp.stack(
+            [
+                over_rows(grad_first * first_unit),
+                over_rows(grad_first),
+                over_rows(grad_branch),
+                over_rows(grad_second * unit),
+                over_rows(grad_second),
+                over_rows(grad_result),
+            ]
+        ),
+        ("dp", "row", "col"),
+    )
+    by_col = lax.psum(
+        jnp.concatenate([over_rows(grad_queries), over_rows(grad_values), over_rows(grad_pre)]), ("dp", "row")
+    )
+    return (
+        result,
+        grad_tokens,
+        shared[0],
+        shared[1],
+        grad_w[:, :head_width],
+        grad_w[:, head_width : 2 * head_width],
+        grad_w[:, 2 * head_width :],
+        by_col[:head_width],
+        by_col[head_width : 2 * head_width],
+        grad_trailing[:head_width],
+        shared[2],
+        shared[3],
+        shared[4],
+        grad_up,
+        by_col[2 * head_width :],
+        grad_trailing[head_width:],
+        shared[5],
+    )
+
+
 def solution(mesh):
     return jax.shard_map(
-        local,
+        local_sequence if fits(mesh) else local_general,
         mesh=mesh,
         in_specs=(
             P(None, ("dp", "row", "col"), None),

time: 2180 us -> 644 us (0.30); the launches traced: 2150 us -> 638 us
  waiting for transfers between devices: 1550 us -> 282 us
  matrix products: 245 us -> 69.9 us
  blocking collectives: 176 us -> 59.7 us
  Pallas kernels: 0 us -> 59.7 us
  starting transfers between devices: 3.82 us -> 35.2 us
  other arithmetic: 89.1 us -> 63.4 us
    reduce_scatter x30 -> x0, waiting for transfers between devices: 1180 us -> none  [the longest x16 449 us: fold_rows(): return lax.psum_scatter(partial_sum, 'col', scatter_dimension=0, tiled=True)]
    all_gather x26 -> x3, waiting for transfers between devices: 358 us -> 8.45 us  [the longest x1 8.45 us: local_sequence(): lax.all_gather(jnp.concatenate([w_output, w_down], axis=0), ('dp', 'row')...]
    ppermute x0 -> x29, waiting for transfers between devices: none -> 221 us  [swap(): lax.ppermute(array, axis, [(place, place ^ flip) for place in range(size)])]
    all_gather x4 -> x0, blocking collectives: 135 us -> none  [the longest x1 35.5 us: fetch_weights(): lax.all_gather(w_query, ('dp', 'row'), axis=0, tiled=True)]
    dot_general x36 -> x0, matrix products: 60.5 us -> none  [the longest x4 15.8 us: output_step(): jnp.einsum('hqk,khd->qhd', weights_low, block_of(value_rows, start, block...]
    pallas_call x0 -> x2, Pallas kernels: none -> 59.7 us  [the longest x1 34.8 us: attention_back(): pl.pallas_call(attention_back_kernel, grid=(pairs, chunks), in_specs=[row...]
    dot_general x24 -> x4, matrix products: 80.8 us -> 24.6 us  [transposed_right(): lax.dot_general(former, latter, (((1,), (1,)), ((), ())), preferred_eleme...]
    all_to_all x0 -> x4, waiting for transfers between devices: none -> 52.7 us  [trade_rows(): return lax.all_to_all(array, 'row', split_axis=0, concat_axis=0)]
  transfers between devices with their start and end apart: 56 -> 36, of which waited for: 46 -> 17; matrix products, arithmetic and copies ran while one was open for 14% -> 23% of each run, Pallas kernels for 0% -> 9%
where the time goes in v1:
time: 644 us; the launch traced here: 638 us
  waiting for transfers between devices  282 us (44%)
  matrix products  69.9 us (11%)
  other arithmetic  63.4 us (10%)
  Pallas kernels  59.7 us (9%)
  blocking collectives  59.7 us (9%)
  local copies, waits for them, and re-layouts  52.8 us (8%)
  starting transfers between devices  35.2 us (5%)
  between operations  14.9 us (2%)
    ppermute x29, waiting for transfers between devices, swap(): lax.ppermute(array, axis, [(place, place ^ flip) for place in range(size)])  221 us
    all_to_all x4, waiting for transfers between devices, trade_rows(): return lax.all_to_all(array, 'row', split_axis=0, concat_axis=0)  52.7 us
    psum x1, blocking collectives, local_sequence(): lax.psum(jnp.stack([over_rows(grad_first * first_unit), over_rows(grad_fi...  37.5 us
    pallas_call x1, Pallas kernels, attention_back(): pl.pallas_call(attention_back_kernel, grid=(pairs, chunks), in_specs=[row...  34.8 us
    pallas_call x1, Pallas kernels, attention_out(): pl.pallas_call(attention_out_kernel, grid=(pairs, chunks), in_specs=[row_...  24.9 us
    dot_general x4, matrix products, transposed_right(): lax.dot_general(former, latter, (((1,), (1,)), ((), ())), preferred_eleme...  24.6 us
    dot_general x4, matrix products, transposed_left(): lax.dot_general(former, latter, (((0,), (0,)), ((), ())), preferred_eleme...  24.1 us
    unnamed x124, local copies, waits for them, and re-layouts  23.9 us
  transfers between devices with their start and end apart: 36, of which 17 were waited for; matrix products, arithmetic and copies ran while one was open for 23% of the time, Pallas kernels for 9%

profile of v1, /device:TPU:0, one launch (start us, length us, event | category | flops | bytes accessed | tf_op | source)
XLA Modules:
  0.0 638.0 jit_solution(11013615056413757815)
XLA Ops:
  7.2 6.3 all-to-all-start
  15.2 30.4 %all-to-all-done = bf16[4,128,1024]{2,1,0:T(8,128)(2,1)S(1)} async-done(((bf16[4,128,1024]{2,1,0:T(8,128)(2,1)}), bf16[4,128,1024]{2,1,0:T(8,128)(2,1)S(1)}, u32[]{:S(2)}, u32[]{:S(2)}) %all-to-all-start) | async-done | bytes 1048608 | tf_op jit(solution)/shard_map/all_to_all | solution.py:571
  47.2 22.4 %collective-permute-done.1 = bf16[4,128,1024]{2,1,0:T(8,128)(2,1)S(1)} collective-permute-done((bf16[4,128,1024]{2,1,0:T(8,128)(2,1)S(1)}, bf16[4,128,1024]{2,1,0:T(8,128)(2,1)S(1)}, u32[]{:S(2)}, u32[]{:S(2)}) %collective-permute-start.1) | collective-permute-done | bytes 1048608 | tf_op jit(solution)/shard_map/ppermute | solution.py:555
  78.9 2.6 multiply_reduce_fusion
  81.5 3.4 fusion.10
  85.0 5.7 fusion.67
  93.5 24.9 %attention_out.1 = (bf16[2048,256]{1,0:T(8,128)(2,1)}, f32[2,4,2,512]{3,2,1,0:T(2,128)}) custom-call(bf16[2048,256]{1,0:T(8,128)(2,1)} %get-tuple-element.49.q_ref, bf16[2048,256]{1,0:T(8,128)(2,1)} %slice.238.k_ref, bf16[2048,256]{1,0:T(8,128)(2,1)} %get-tuple-element.48.v_ref, f32[1,2048]{1,0:T(1,128)} %bitcast.156, f32[512,512]{1,0:T(8,128)} %get-tuple-element.66.causal_ref), custom_call_target="tpu_custom_call" | custom-call | flops 40000000000 | bytes 4000000 | tf_op jit(solution)/shard_map/attention_out/pallas_call | solution.py:460
  118.4 8.5 %all-gather.6.cloned.1.call-done = bf16[1280,1024]{1,0:T(8,128)(2,1)} async-done(((bf16[1280,128]{1,0:T(8,128)(2,1)}), bf16[1280,1024]{1,0:T(8,128)(2,1)}) %all-gather.6.cloned.1.call-update) | async-done | bytes 2621456 | tf_op jit(solution)/shard_map/all_gather | solution.py:642
  126.9 2.6 fusion.50
  129.5 3.2 fusion.63
  134.9 3.5 all-to-all-start.2
  138.5 3.9 collective-permute-done.3
  142.4 4.4 copy_add_fusion.3
  151.3 22.3 %all-to-all-done.2 = bf16[4,128,1024]{2,1,0:T(8,128)(2,1)S(1)} async-done(((bf16[4,128,1024]{2,1,0:T(8,128)(2,1)}), bf16[4,128,1024]{2,1,0:T(8,128)(2,1)S(1)}, u32[]{:S(2)}, u32[]{:S(2)}) %all-to-all-start.2) | async-done | bytes 1048608 | tf_op jit(solution)/shard_map/all_to_all | solution.py:571
  175.6 2.8 fusion.59
  179.8 20.1 %collective-permute-done.11 = bf16[4,128,1024]{2,1,0:T(8,128)(2,1)S(1)} collective-permute-done((bf16[4,128,1024]{2,1,0:T(8,128)(2,1)S(1)}, bf16[4,128,1024]{2,1,0:T(8,128)(2,1)S(1)}, u32[]{:S(2)}, u32[]{:S(2)}) %collective-permute-start.11) | collective-permute-done | bytes 1048608 | tf_op jit(solution)/shard_map/ppermute | solution.py:555
  200.4 20.4 %collective-permute-done.6 = bf16[4,128,1024]{2,1,0:T(8,128)(2,1)S(1)} collective-permute-done((bf16[4,128,1024]{2,1,0:T(8,128)(2,1)S(1)}, bf16[4,128,1024]{2,1,0:T(8,128)(2,1)S(1)}, u32[]{:S(2)}, u32[]{:S(2)}) %collective-permute-start.6) | collective-permute-done | bytes 1048608 | tf_op jit(solution)/shard_map/ppermute | solution.py:555
  227.7 7.1 %fusion.68 = f32[2048,1024]{1,0:T(8,128)S(1)} fusion(bf16[2048,1024]{1,0:T(8,128)(2,1)} %bitcast.144, bf16[1024,1024]{1,0:T(8,128)(2,1)} %all-gather.8.cloned.1.call-done), kind=kOutput, calls=%fused_computation.151 | convolution fusion | flops 4294967296 | bytes 14680064 | tf_op jit(solution)/shard_map/dot_general | solution.py:28
  234.8 5.8 fusion.41
  240.7 3.3 fusion.62
  244.0 2.4 copy.61
  247.7 12.7 %convert_reduce_fusion = (f32[1024]{0:T(1024)}, bf16[2048,1024]{1,0:T(8,128)(2,1)S(1)}) fusion(f32[2048,1024]{1,0:T(8,128)} %copy-done.56, f32[1024]{0:T(1024)S(1)} %copy-done.53, bf16[2048,1024]{1,0:T(8,128)(2,1)S(1)} %bitcast.142, bf16[1280,1024]{1,0:T(8,128)(2,1)S(1)} %copy-done.26), kind=kOutput, calls=%fused_computation.14 | convolution fusion | flops 4343200768 | bytes 18882560 | tf_op jit(solution)/shard_map/dot_general | solution.py:38
  260.4 4.6 fusion.69
  265.0 3.3 fusion.61
  271.1 4.5 copy_add_fusion.2
  278.2 3.3 copy_add_fusion.1
  283.2 4.8 fusion.73
  288.1 35.4 %collective-permute-done.14 = bf16[4,128,1024]{2,1,0:T(8,128)(2,1)S(1)} collective-permute-done((bf16[4,128,1024]{2,1,0:T(8,128)(2,1)S(1)}, bf16[4,128,1024]{2,1,0:T(8,128)(2,1)S(1)}, u32[]{:S(2)}, u32[]{:S(2)}) %collective-permute-start.14) | collective-permute-done | bytes 1048608 | tf_op jit(solution)/shard_map/ppermute | solution.py:555
  325.4 2.9 convert_reduce_fusion.4
  332.4 20.5 %collective-permute-done.16 = bf16[4,128,1024]{2,1,0:T(8,128)(2,1)} collective-permute-done((bf16[4,128,1024]{2,1,0:T(8,128)(2,1)}, bf16[4,128,1024]{2,1,0:T(8,128)(2,1)}, u32[]{:S(2)}, u32[]{:S(2)}) %collective-permute-start.16) | collective-permute-done | bytes 1048608 | tf_op jit(solution)/shard_map/ppermute | solution.py:555
  361.6 21.0 %collective-permute-done.27 = bf16[256,1024]{1,0:T(8,128)(2,1)} collective-permute-done((bf16[256,1024]{1,0:T(8,128)(2,1)}, bf16[256,1024]{1,0:T(8,128)(2,1)}, u32[]{:S(2)}, u32[]{:S(2)}) %collective-permute-start.27) | collective-permute-done | bytes 524320 | tf_op jit(solution)/shard_map/ppermute | solution.py:555
  385.9 4.5 all-to-all-start.1
  393.4 3.7 convolution_convert_fusion.do_ref
  397.1 34.8 %attention_back.1 = (bf16[2048,256]{1,0:T(8,128)(2,1)}, bf16[2048,256]{1,0:T(8,128)(2,1)}, bf16[2048,256]{1,0:T(8,128)(2,1)}) custom-call(bf16[2048,256]{1,0:T(8,128)(2,1)} %get-tuple-element.49.q_ref, bf16[2048,256]{1,0:T(8,128)(2,1)} %slice.238.k_ref, bf16[2048,256]{1,0:T(8,128)(2,1)} %get-tuple-element.48.v_ref, ...), custom_call_target="tpu_custom_call" | custom-call | flops 80000000000 | bytes 6000000 | tf_op jit(solution)/shard_map/attention_back/pallas_call | solution.py:531
  434.8 3.5 fusion.70
  438.3 3.2 fusion.60
  445.3 11.4 %fusion.56 = f32[1024,1024]{1,0:T(8,128)} fusion(bf16[2048,1024]{1,0:T(8,128)(2,1)S(1)} %bitcast.143, f32[2048,1024]{1,0:T(8,128)} %copy-done.56, f32[1024]{0:T(1024)S(1)} %copy-done.53), kind=kOutput, calls=%fused_computation.141 | convolution fusion | flops 4315938816 | bytes 16781312 | tf_op jit(solution)/shard_map/dot_general | solution.py:32
  460.6 22.2 %psum.15 = f32[1536]{0:T(1024)S(1)} all-reduce(f32[1536]{0:T(1024)S(1)} %pad_maximum_fusion.5), channel_id=1, replica_groups=mesh['dp'=2,'row'=4,'col'=4] {'dp','row'}, use_global_device_ids=true, to_apply=%region_20.21 | all-reduce | flops 1536 | bytes 12288 | tf_op jit(solution)/shard_map/psum | solution.py:713
  483.5 6.5 %fusion.71 = f32[1024,768]{1,0:T(8,128)S(1)} fusion(bf16[2048,1024]{1,0:T(8,128)(2,1)} %fusion.10, bf16[2048,768]{1,0:T(8,128)(2,1)} %copy-done.25), kind=kOutput, calls=%fused_computation.154 | convolution fusion | flops 3221225472 | bytes 10485760 | tf_op jit(solution)/shard_map/dot_general | solution.py:32
  494.4 16.3 %collective-permute-done.20 = bf16[512,768]{1,0:T(8,128)(2,1)S(1)} collective-permute-done((bf16[512,768]{1,0:T(8,128)(2,1)S(1)}, bf16[512,768]{1,0:T(8,128)(2,1)S(1)}, u32[]{:S(2)}, u32[]{:S(2)}) %collective-permute-start.20) | collective-permute-done | bytes 786464 | tf_op jit(solution)/shard_map/ppermute | solution.py:555
  511.0 3.1 copy_add_fusion
  515.8 6.5 %collective-permute-done.21 = bf16[256,768]{1,0:T(8,128)(2,1)S(1)} collective-permute-done((bf16[256,768]{1,0:T(8,128)(2,1)S(1)}, bf16[256,768]{1,0:T(8,128)(2,1)S(1)}, u32[]{:S(2)}, u32[]{:S(2)}) %collective-permute-start.21) | collective-permute-done | bytes 393248 | tf_op jit(solution)/shard_map/ppermute | solution.py:555
  522.6 10.7 %collective-permute-done.23 = bf16[1280,512]{1,0:T(8,128)(2,1)S(1)} collective-permute-done((bf16[1280,512]{1,0:T(8,128)(2,1)S(1)}, bf16[1280,512]{1,0:T(8,128)(2,1)S(1)}, u32[]{:S(2)}, u32[]{:S(2)}) %collective-permute-start.23) | collective-permute-done | bytes 1310752 | tf_op jit(solution)/shard_map/ppermute | solution.py:555
  536.6 3.3 fusion.37
  539.8 4.2 all-to-all-start.3
  544.0 27.3 %collective-permute-done.24 = bf16[1280,256]{1,0:T(8,128)(2,1)} collective-permute-done((bf16[1280,256]{1,0:T(8,128)(2,1)}, bf16[1280,256]{1,0:T(8,128)(2,1)}, u32[]{:S(2)}, u32[]{:S(2)}) %collective-permute-start.24) | collective-permute-done | bytes 655392 | tf_op jit(solution)/shard_map/ppermute | solution.py:555
  575.0 13.3 %collective-permute-done.25 = bf16[1280,128]{1,0:T(8,128)(2,1)S(1)} collective-permute-done((bf16[1280,128]{1,0:T(8,128)(2,1)S(1)}, bf16[1280,128]{1,0:T(8,128)(2,1)S(1)}, u32[]{:S(2)}, u32[]{:S(2)}) %collective-permute-start.25) | collective-permute-done | bytes 327712 | tf_op jit(solution)/shard_map/ppermute | solution.py:555
  589.9 37.5 %psum.14 = f32[6,1024]{1,0:T(8,128)S(1)} all-reduce(f32[6,1024]{1,0:T(8,128)S(1)} %stack.107), channel_id=1, replica_groups=mesh['dp'=2,'row'=4,'col'=4] {'dp','row','col'}, use_global_device_ids=true, to_apply=%region_16.17 | all-reduce | flops 6144 | bytes 49152 | tf_op jit(solution)/shard_map/psum | solution.py:700
  (250 shorter events, 91.6 us)
Async XLA Ops:
  7.2 64.1 %copy-start = (s32[1,4]{1,0:T(1,128)S(1)}, s32[1,4]{1,0:T(1,128)}, u32[]{:S(2)}) copy-start(s32[1,4]{1,0:T(1,128)} %param.19) | copy-start | bytes 52
  7.2 38.4 %all-to-all-start = ((bf16[4,128,1024]{2,1,0:T(8,128)(2,1)}), bf16[4,128,1024]{2,1,0:T(8,128)(2,1)S(1)}, u32[]{:S(2)}, u32[]{:S(2)}) async-start(bf16[4,128,1024]{2,1,0:T(8,128)(2,1)} %param.18), calls=%async_computation | async-start | bytes 2097152 | tf_op jit(solution)/shard_map/all_to_all | solution.py:571
  13.5 71.4 %all-gather.4.cloned.1.call-start = ((), (), s32[]{:S(2)}) async-start(), calls=%async_computation.4 | async-start | bytes 1769472 | tf_op jit(solution)/shard_map/all_gather | solution.py:639
  15.2 111.7 %all-gather.6.cloned.1.call-start = ((), (), s32[]{:S(2)}) async-start(), calls=%async_computation.5 | async-start | bytes 2949120 | tf_op jit(solution)/shard_map/all_gather | solution.py:642
  45.6 129.9 %copy-start.2 = (bf16[4,128,1024]{2,1,0:T(8,128)(2,1)}, bf16[4,128,1024]{2,1,0:T(8,128)(2,1)S(1)}, u32[]{:S(2)}) copy-start(bf16[4,128,1024]{2,1,0:T(8,128)(2,1)S(1)} %all-to-all-done) | copy-start | bytes 3145732
  45.6 23.9 %collective-permute-start.1 = (bf16[4,128,1024]{2,1,0:T(8,128)(2,1)S(1)}, bf16[4,128,1024]{2,1,0:T(8,128)(2,1)S(1)}, u32[]{:S(2)}, u32[]{:S(2)}) collective-permute-start(bf16[4,128,1024]{2,1,0:T(8,128)(2,1)S(1)} %all-to-all-done), channel_id=1, source_target_pairs={{0,2},{1,3},{2,0},{3,1},{4,6},{5,7},{6,4},{7,5},{8,10},{9,11},{10,... | collective-permute-start | bytes 3145736 | tf_op jit(solution)/shard_map/ppermute | solution.py:555
  47.2 27.7 %collective-permute-start = (bf16[4,128,1024]{2,1,0:T(8,128)(2,1)S(1)}, bf16[4,128,1024]{2,1,0:T(8,128)(2,1)}, u32[]{:S(2)}, u32[]{:S(2)}) collective-permute-start(bf16[4,128,1024]{2,1,0:T(8,128)(2,1)S(1)} %all-to-all-done), channel_id=1, source_target_pairs={{0,1},{1,0},{2,3},{3,2},{4,5},{5,4},{6,7},{7,6},{8,9},{9,8},{10,11... | collective-permute-start | bytes 3145736 | tf_op jit(solution)/shard_map/ppermute | solution.py:555
  69.6 5.3 collective-permute-start.2
  134.9 7.5 %collective-permute-start.3 = (f32[4,2,128,1024]{3,2,0,1:T(8,128)}, f32[4,2,128,1024]{3,2,0,1:T(8,128)}, u32[]{:S(2)}, u32[]{:S(2)}) collective-permute-start(f32[4,2,128,1024]{3,2,0,1:T(8,128)} %copy.59), channel_id=1, source_target_pairs={{0,1},{1,0},{2,3},{3,2},{4,5},{5,4},{6,7},{7,6},{8,9},{9,8},{10,11... | collective-permute-start | bytes 12582920 | tf_op jit(solution)/shard_map/ppermute | solution.py:555
  134.9 38.6 %all-to-all-start.2 = ((bf16[4,128,1024]{2,1,0:T(8,128)(2,1)}), bf16[4,128,1024]{2,1,0:T(8,128)(2,1)S(1)}, u32[]{:S(2)}, u32[]{:S(2)}) async-start(bf16[4,128,1024]{2,1,0:T(8,128)(2,1)} %param.35), calls=%async_computation.2 | async-start | bytes 2097152 | tf_op jit(solution)/shard_map/all_to_all | solution.py:571
  138.5 89.2 %all-gather.8.cloned.1.call-start = ((), (), s32[]{:S(2)}) async-start(), calls=%async_computation.6 | async-start | bytes 2359296 | tf_op jit(solution)/shard_map/all_gather | solution.py:644
  149.0 26.6 %collective-permute-start.4 = (bf16[4,128,1024]{2,1,0:T(8,128)(2,1)S(1)}, bf16[4,128,1024]{2,1,0:T(8,128)(2,1)}, u32[]{:S(2)}, u32[]{:S(2)}) collective-permute-start(bf16[4,128,1024]{2,1,0:T(8,128)(2,1)S(1)} %fusion.45), channel_id=1, source_target_pairs={{0,2},{1,3},{2,0},{3,1},{4,6},{5,7},{6,4},{7,5},{8,10},{9,11},{10,... | collective-permute-start | bytes 3145736 | tf_op jit(solution)/shard_map/ppermute | solution.py:555
  173.8 26.2 %collective-permute-start.11 = (bf16[4,128,1024]{2,1,0:T(8,128)(2,1)S(1)}, bf16[4,128,1024]{2,1,0:T(8,128)(2,1)S(1)}, u32[]{:S(2)}, u32[]{:S(2)}) collective-permute-start(bf16[4,128,1024]{2,1,0:T(8,128)(2,1)S(1)} %fusion.38), channel_id=1, source_target_pairs={{0,2},{1,3},{2,0},{3,1},{4,6},{5,7},{6,4},{7,5},{8,10},{9,11},{10,... | collective-permute-start | bytes 3145736 | tf_op jit(solution)/shard_map/ppermute | solution.py:555
  178.4 42.5 %copy-start.5 = (bf16[4,128,1024]{2,1,0:T(8,128)(2,1)S(1)}, bf16[4,128,1024]{2,1,0:T(8,128)(2,1)}, u32[]{:S(2)}) copy-start(bf16[4,128,1024]{2,1,0:T(8,128)(2,1)} %copy-done.4) | copy-start | bytes 3145732
  179.2 41.7 %collective-permute-start.6 = (bf16[4,128,1024]{2,1,0:T(8,128)(2,1)S(1)}, bf16[4,128,1024]{2,1,0:T(8,128)(2,1)S(1)}, u32[]{:S(2)}, u32[]{:S(2)}) collective-permute-start(bf16[4,128,1024]{2,1,0:T(8,128)(2,1)S(1)} %add_convert_fusion), channel_id=1, source_target_pairs={{0,2},{1,3},{2,0},{3,1},{4,6},{5,7},{6,4},{7,5},{8,10},{9,11},{10,... | collective-permute-start | bytes 3145736 | tf_op jit(solution)/shard_map/ppermute | solution.py:555
  179.8 41.3 %collective-permute-start.10 = (bf16[4,128,1024]{2,1,0:T(8,128)(2,1)S(1)}, bf16[4,128,1024]{2,1,0:T(8,128)(2,1)S(1)}, u32[]{:S(2)}, u32[]{:S(2)}) collective-permute-start(bf16[4,128,1024]{2,1,0:T(8,128)(2,1)S(1)} %fusion.38), channel_id=1, source_target_pairs={{0,1},{1,0},{2,3},{3,2},{4,5},{5,4},{6,7},{7,6},{8,9},{9,8},{10,11... | collective-permute-start | bytes 3145736 | tf_op jit(solution)/shard_map/ppermute | solution.py:555
  199.9 21.2 %collective-permute-start.12 = (bf16[4,128,1024]{2,1,0:T(8,128)(2,1)S(1)}, bf16[4,128,1024]{2,1,0:T(8,128)(2,1)S(1)}, u32[]{:S(2)}, u32[]{:S(2)}) collective-permute-start(bf16[4,128,1024]{2,1,0:T(8,128)(2,1)S(1)} %collective-permute-done.11), channel_id=1, source_target_pairs={{0,1},{1,0},{2,3},{3,2},{4,5},{5,4},{6,7},{7,6},{8,9},{9,8},{10,11... | collective-permute-start | bytes 3145736 | tf_op jit(solution)/shard_map/ppermute | solution.py:555
  199.9 24.7 %collective-permute-start.5 = (bf16[4,128,1024]{2,1,0:T(8,128)(2,1)S(1)}, bf16[4,128,1024]{2,1,0:T(8,128)(2,1)S(1)}, u32[]{:S(2)}, u32[]{:S(2)}) collective-permute-start(bf16[4,128,1024]{2,1,0:T(8,128)(2,1)S(1)} %add_convert_fusion), channel_id=1, source_target_pairs={{0,1},{1,0},{2,3},{3,2},{4,5},{5,4},{6,7},{7,6},{8,9},{9,8},{10,11... | collective-permute-start | bytes 3145736 | tf_op jit(solution)/shard_map/ppermute | solution.py:555
  220.9 3.8 collective-permute-start.7
  246.4 24.7 %collective-permute-start.8 = (f32[4,2,128,1024]{3,2,0,1:T(8,128)}, f32[4,2,128,1024]{3,2,0,1:T(8,128)}, u32[]{:S(2)}, u32[]{:S(2)}) collective-permute-start(f32[4,2,128,1024]{3,2,0,1:T(8,128)} %copy.61), channel_id=1, source_target_pairs={{0,1},{1,0},{2,3},{3,2},{4,5},{5,4},{6,7},{7,6},{8,9},{9,8},{10,11... | collective-permute-start | bytes 12582920 | tf_op jit(solution)/shard_map/ppermute | solution.py:555
  270.6 7.6 %collective-permute-start.13 = (f32[4,2,128,1024]{3,2,0,1:T(8,128)}, f32[4,2,128,1024]{3,2,0,1:T(8,128)}, u32[]{:S(2)}, u32[]{:S(2)}) collective-permute-start(f32[4,2,128,1024]{3,2,0,1:T(8,128)} %copy.63), channel_id=1, source_target_pairs={{0,1},{1,0},{2,3},{3,2},{4,5},{5,4},{6,7},{7,6},{8,9},{9,8},{10,11... | collective-permute-start | bytes 12582920 | tf_op jit(solution)/shard_map/ppermute | solution.py:555
  275.8 49.5 %collective-permute-start.9 = (bf16[4,128,1024]{2,1,0:T(8,128)(2,1)S(1)}, bf16[4,128,1024]{2,1,0:T(8,128)(2,1)S(1)}, u32[]{:S(2)}, u32[]{:S(2)}) collective-permute-start(bf16[4,128,1024]{2,1,0:T(8,128)(2,1)S(1)} %fusion.46), channel_id=1, source_target_pairs={{0,2},{1,3},{2,0},{3,1},{4,6},{5,7},{6,4},{7,5},{8,10},{9,11},{10,... | collective-permute-start | bytes 3145736 | tf_op jit(solution)/shard_map/ppermute | solution.py:555
  281.7 41.8 %collective-permute-start.14 = (bf16[4,128,1024]{2,1,0:T(8,128)(2,1)S(1)}, bf16[4,128,1024]{2,1,0:T(8,128)(2,1)S(1)}, u32[]{:S(2)}, u32[]{:S(2)}) collective-permute-start(bf16[4,128,1024]{2,1,0:T(8,128)(2,1)S(1)} %fusion.47), channel_id=1, source_target_pairs={{0,2},{1,3},{2,0},{3,1},{4,6},{5,7},{6,4},{7,5},{8,10},{9,11},{10,... | collective-permute-start | bytes 3145736 | tf_op jit(solution)/shard_map/ppermute | solution.py:555
  288.1 41.8 %copy-start.23 = (f32[1024,1024]{1,0:T(8,128)}, f32[1024,1024]{1,0:T(8,128)S(1)}, u32[]{:S(2)}) copy-start(f32[1024,1024]{1,0:T(8,128)S(1)} %fusion.73) | copy-start | bytes 12582916
  288.1 37.3 %copy-start.46 = (f32[1024]{0:T(1024)S(1)}, f32[1024]{0:T(1024)}, u32[]{:S(2)}) copy-start(f32[1024]{0:T(1024)} %param.34) | copy-start | bytes 12292
  328.3 24.6 %collective-permute-start.16 = (bf16[4,128,1024]{2,1,0:T(8,128)(2,1)}, bf16[4,128,1024]{2,1,0:T(8,128)(2,1)}, u32[]{:S(2)}, u32[]{:S(2)}) collective-permute-start(bf16[4,128,1024]{2,1,0:T(8,128)(2,1)} %get-tuple-element.36), channel_id=1, source_target_pairs={{0,2},{1,3},{2,0},{3,1},{4,6},{5,7},{6,4},{7,5},{8,10},{9,11},{10,... | collective-permute-start | bytes 3145736 | tf_op jit(solution)/shard_map/ppermute | solution.py:555
  331.0 24.3 %collective-permute-start.26 = (bf16[512,1024]{1,0:T(8,128)(2,1)}, bf16[512,1024]{1,0:T(8,128)(2,1)}, u32[]{:S(2)}, u32[]{:S(2)}) collective-permute-start(bf16[512,1024]{1,0:T(8,128)(2,1)} %dynamic-slice_convert_fusion), channel_id=1, source_target_pairs={{0,16},{16,0},{1,17},{17,1},{2,18},{18,2},{3,19},{19,3},{4,20},{20... | collective-permute-start | bytes 3145736 | tf_op jit(solution)/shard_map/ppermute | solution.py:555
  332.4 58.0 %collective-permute-start.15 = (bf16[4,128,1024]{2,1,0:T(8,128)(2,1)}, bf16[4,128,1024]{2,1,0:T(8,128)(2,1)}, u32[]{:S(2)}, u32[]{:S(2)}) collective-permute-start(bf16[4,128,1024]{2,1,0:T(8,128)(2,1)} %get-tuple-element.36), channel_id=1, source_target_pairs={{0,1},{1,0},{2,3},{3,2},{4,5},{5,4},{6,7},{7,6},{8,9},{9,8},{10,11... | collective-permute-start | bytes 3145736 | tf_op jit(solution)/shard_map/ppermute | solution.py:555
  352.9 37.4 %collective-permute-start.17 = (bf16[4,128,1024]{2,1,0:T(8,128)(2,1)}, bf16[4,128,1024]{2,1,0:T(8,128)(2,1)}, u32[]{:S(2)}, u32[]{:S(2)}) collective-permute-start(bf16[4,128,1024]{2,1,0:T(8,128)(2,1)} %collective-permute-done.16), channel_id=1, source_target_pairs={{0,1},{1,0},{2,3},{3,2},{4,5},{5,4},{6,7},{7,6},{8,9},{9,8},{10,11... | collective-permute-start | bytes 3145736 | tf_op jit(solution)/shard_map/ppermute | solution.py:555
  359.7 22.9 %collective-permute-start.27 = (bf16[256,1024]{1,0:T(8,128)(2,1)}, bf16[256,1024]{1,0:T(8,128)(2,1)}, u32[]{:S(2)}, u32[]{:S(2)}) collective-permute-start(bf16[256,1024]{1,0:T(8,128)(2,1)} %dynamic-slice_convert_fusion.3), channel_id=1, source_target_pairs={{0,8},{4,12},{8,0},{12,4},{1,9},{5,13},{9,1},{13,5},{2,10},{6,14},... | collective-permute-start | bytes 1572872 | tf_op jit(solution)/shard_map/ppermute | solution.py:555
  385.8 70.9 %collective-permute-start.28 = (bf16[128,1024]{1,0:T(8,128)(2,1)}, bf16[128,1024]{1,0:T(8,128)(2,1)S(1)}, u32[]{:S(2)}, u32[]{:S(2)}) collective-permute-start(bf16[128,1024]{1,0:T(8,128)(2,1)} %dynamic-slice_convert_fusion.6), channel_id=1, source_target_pairs={{0,4},{4,0},{8,12},{12,8},{1,5},{5,1},{9,13},{13,9},{2,6},{6,2},{1... | collective-permute-start | bytes 786440 | tf_op jit(solution)/shard_map/ppermute | solution.py:555
  385.9 71.8 %all-to-all-start.1 = ((bf16[4,128,1024]{2,1,0:T(8,128)(2,1)}), bf16[4,128,1024]{2,1,0:T(8,128)(2,1)}, u32[]{:S(2)}, u32[]{:S(2)}) async-start(bf16[4,128,1024]{2,1,0:T(8,128)(2,1)} %get-tuple-element.50), calls=%async_computation.1 | async-start | bytes 2097152 | tf_op jit(solution)/shard_map/all_to_all | solution.py:571
  444.0 66.9 %collective-permute-start.18 = (f32[4,2,128,1024]{3,2,0,1:T(8,128)}, f32[4,2,128,1024]{3,2,0,1:T(8,128)}, u32[]{:S(2)}, u32[]{:S(2)}) collective-permute-start(f32[4,2,128,1024]{3,2,0,1:T(8,128)} %copy.65), channel_id=1, source_target_pairs={{0,1},{1,0},{2,3},{3,2},{4,5},{5,4},{6,7},{7,6},{8,9},{9,8},{10,11... | collective-permute-start | bytes 12582920 | tf_op jit(solution)/shard_map/ppermute | solution.py:555
  490.1 20.5 %collective-permute-start.20 = (bf16[512,768]{1,0:T(8,128)(2,1)S(1)}, bf16[512,768]{1,0:T(8,128)(2,1)S(1)}, u32[]{:S(2)}, u32[]{:S(2)}) collective-permute-start(bf16[512,768]{1,0:T(8,128)(2,1)S(1)} %dynamic-slice_convert_fusion.1), channel_id=1, source_target_pairs={{0,16},{16,0},{1,17},{17,1},{2,18},{18,2},{3,19},{19,3},{4,20},{20... | collective-permute-start | bytes 2359304 | tf_op jit(solution)/shard_map/ppermute | solution.py:555
  492.4 40.9 %collective-permute-start.23 = (bf16[1280,512]{1,0:T(8,128)(2,1)S(1)}, bf16[1280,512]{1,0:T(8,128)(2,1)S(1)}, u32[]{:S(2)}, u32[]{:S(2)}) collective-permute-start(bf16[1280,512]{1,0:T(8,128)(2,1)S(1)} %fusion.12), channel_id=1, source_target_pairs={{0,16},{16,0},{1,17},{17,1},{2,18},{18,2},{3,19},{19,3},{4,20},{20... | collective-permute-start | bytes 3932168 | tf_op jit(solution)/shard_map/ppermute | solution.py:555
  510.9 11.4 %collective-permute-start.21 = (bf16[256,768]{1,0:T(8,128)(2,1)S(1)}, bf16[256,768]{1,0:T(8,128)(2,1)S(1)}, u32[]{:S(2)}, u32[]{:S(2)}) collective-permute-start(bf16[256,768]{1,0:T(8,128)(2,1)S(1)} %dynamic-slice_convert_fusion.4), channel_id=1, source_target_pairs={{0,8},{4,12},{8,0},{12,4},{1,9},{5,13},{9,1},{13,5},{2,10},{6,14},... | collective-permute-start | bytes 1179656 | tf_op jit(solution)/shard_map/ppermute | solution.py:555
  514.3 20.5 %collective-permute-start.19 = (bf16[4,128,1024]{2,1,0:T(8,128)(2,1)S(1)}, bf16[4,128,1024]{2,1,0:T(8,128)(2,1)S(1)}, u32[]{:S(2)}, u32[]{:S(2)}) collective-permute-start(bf16[4,128,1024]{2,1,0:T(8,128)(2,1)S(1)} %fusion.48), channel_id=1, source_target_pairs={{0,2},{1,3},{2,0},{3,1},{4,6},{5,7},{6,4},{7,5},{8,10},{9,11},{10,... | collective-permute-start | bytes 3145736 | tf_op jit(solution)/shard_map/ppermute | solution.py:555
  522.5 50.7 %collective-permute-start.22 = (bf16[128,768]{1,0:T(8,128)(2,1)S(1)}, bf16[128,768]{1,0:T(8,128)(2,1)S(1)}, u32[]{:S(2)}, u32[]{:S(2)}) collective-permute-start(bf16[128,768]{1,0:T(8,128)(2,1)S(1)} %dynamic-slice_convert_fusion.7), channel_id=1, source_target_pairs={{0,4},{4,0},{8,12},{12,8},{1,5},{5,1},{9,13},{13,9},{2,6},{6,2},{1... | collective-permute-start | bytes 589832 | tf_op jit(solution)/shard_map/ppermute | solution.py:555
  534.7 36.6 %collective-permute-start.24 = (bf16[1280,256]{1,0:T(8,128)(2,1)}, bf16[1280,256]{1,0:T(8,128)(2,1)}, u32[]{:S(2)}, u32[]{:S(2)}) collective-permute-start(bf16[1280,256]{1,0:T(8,128)(2,1)} %dynamic-slice_convert_fusion.2), channel_id=1, source_target_pairs={{0,8},{4,12},{8,0},{12,4},{1,9},{5,13},{9,1},{13,5},{2,10},{6,14},... | collective-permute-start | bytes 1966088 | tf_op jit(solution)/shard_map/ppermute | solution.py:555
  539.8 88.2 %all-to-all-start.3 = ((bf16[4,128,1024]{2,1,0:T(8,128)(2,1)}), bf16[4,128,1024]{2,1,0:T(8,128)(2,1)S(1)}, u32[]{:S(2)}, u32[]{:S(2)}) async-start(bf16[4,128,1024]{2,1,0:T(8,128)(2,1)} %get-tuple-element.52), calls=%async_computation.3 | async-start | bytes 2097152 | tf_op jit(solution)/shard_map/all_to_all | solution.py:571
  544.0 45.8 %copy-start.39 = (f32[1024]{0:T(1024)S(1)}, f32[1024]{0:T(1024)}, u32[]{:S(2)}) copy-start(f32[1024]{0:T(1024)} %get-tuple-element.31) | copy-start | bytes 12292
  544.0 45.8 %copy-start.40 = (f32[1024]{0:T(1024)S(1)}, f32[1024]{0:T(1024)}, u32[]{:S(2)}) copy-start(f32[1024]{0:T(1024)} %get-tuple-element.34) | copy-start | bytes 12292
  544.0 45.8 %copy-start.41 = (f32[1024]{0:T(1024)S(1)}, f32[1024]{0:T(1024)}, u32[]{:S(2)}) copy-start(f32[1024]{0:T(1024)} %get-tuple-element.35) | copy-start | bytes 12292
  544.0 45.8 %copy-start.42 = (f32[1024]{0:T(1024)S(1)}, f32[1024]{0:T(1024)}, u32[]{:S(2)}) copy-start(f32[1024]{0:T(1024)} %get-tuple-element.27) | copy-start | bytes 12292
  544.0 45.8 %copy-start.43 = (f32[1024]{0:T(1024)S(1)}, f32[1024]{0:T(1024)}, u32[]{:S(2)}) copy-start(f32[1024]{0:T(1024)} %get-tuple-element.30) | copy-start | bytes 12292
  544.0 45.8 %copy-start.44 = (f32[1024]{0:T(1024)S(1)}, f32[1024]{0:T(1024)}, u32[]{:S(2)}) copy-start(f32[1024]{0:T(1024)} %get-tuple-element.51) | copy-start | bytes 12292
  573.1 15.2 %collective-permute-start.25 = (bf16[1280,128]{1,0:T(8,128)(2,1)S(1)}, bf16[1280,128]{1,0:T(8,128)(2,1)S(1)}, u32[]{:S(2)}, u32[]{:S(2)}) collective-permute-start(bf16[1280,128]{1,0:T(8,128)(2,1)S(1)} %dynamic-slice_convert_fusion.5), channel_id=1, source_target_pairs={{0,4},{4,0},{8,12},{12,8},{1,5},{5,1},{9,13},{13,9},{2,6},{6,2},{1... | collective-permute-start | bytes 983048 | tf_op jit(solution)/shard_map/ppermute | solution.py:555
  573.1 58.1 %copy-start.1 = (s32[1,4]{1,0:T(1,128)S(1)}, s32[1,4]{1,0:T(1,128)}, u32[]{:S(2)}) copy-start(s32[1,4]{1,0:T(1,128)} %param.19) | copy-start | bytes 52
  (45 other events, 316.4 us)
Sparse Core Ops, SparseCore 0:
  17.0 51.4 all-gather.3
  71.4 55.3 all-gather.5
  150.7 50.1 all-gather.7

commit v2 on v1

--- a/solution.py
+++ b/solution.py
@@ -555,10 +555,14 @@
     return lax.ppermute(array, axis, [(place, place ^ flip) for place in range(size)])
 
 
-def gather_rows(own):
+def gather_parts(own):
     core = swap(own, "col", 1)
     far = swap(own, "col", 2)
-    return jnp.stack([own, core, far, swap(far, "col", 1)], axis=1)
+    return own, core, far, swap(far, "col", 1)
+
+
+def gather_rows(own):
+    return jnp.stack(gather_parts(own), axis=1)
 
 
 def scatter_rows(partial_sum):
@@ -574,7 +578,7 @@
 def scatter_blocks(gradient, dim):
     dp_place = lax.axis_index("dp")
     row_place = lax.axis_index("row")
-    total = gradient
+    total = gradient.astype(F32)
     for axis, flip, place in (("dp", 1, dp_place), ("row", 2, row_place // 2), ("row", 1, row_place % 2)):
         half = total.shape[dim] // 2
         mine = lax.dynamic_slice_in_dim(total, place * half, half, dim)
@@ -594,6 +598,297 @@
     mean_inner = jnp.mean(inner, axis=-1, keepdims=True)
     mean_unit = jnp.mean(inner * unit, axis=-1, keepdims=True)
     return scale * (inner - mean_inner - unit * mean_unit)
+
+
+GELU_SCALE = 0.7978845608028654
+GELU_CUBE = 0.044715
+
+
+def gelu_parts(values):
+    square = values * values
+    curve = jnp.tanh(GELU_SCALE * values * (1.0 + GELU_CUBE * square))
+    half = 0.5 + 0.5 * curve
+    slope = half + 0.5 * values * (1.0 - curve * curve) * (GELU_SCALE * (1.0 + 3.0 * GELU_CUBE * square))
+    return values * half, slope
+
+
+def peers():
+    place = lax.axis_index("col")
+    return {"col": place + 1 - 2 * (place % 2)}, {"col": (place + 2) % 4}
+
+
+def greet(devices):
+    barrier = pltpu.get_barrier_semaphore()
+    for device in devices:
+        pl.semaphore_signal(barrier, inc=1, device_id=device, device_id_type=pl.DeviceIdType.MESH)
+    pl.semaphore_wait(barrier, len(devices))
+
+
+def remote(source, target, send_sem, recv_sem, device):
+    return pltpu.make_async_remote_copy(
+        src_ref=source,
+        dst_ref=target,
+        send_sem=send_sem,
+        recv_sem=recv_sem,
+        device_id=device,
+        device_id_type=pl.DeviceIdType.MESH,
+    )
+
+
+def feed_kernel(
+    att_ref,
+    wo_ref,
+    wu_ref,
+    wd_ref,
+    tok_ref,
+    g0_ref,
+    g1_ref,
+    g2_ref,
+    g3_ref,
+    vec_ref,
+    bias_up_ref,
+    result_ref,
+    gatt_ref,
+    gmid_ref,
+    gout_ref,
+    gup_ref,
+    gdown_ref,
+    sums_ref,
+    sum_up_ref,
+    g_all,
+    kept,
+    kept_q,
+    core_out,
+    core_in,
+    core_in_q,
+    far_out,
+    far_in,
+    far_out_q,
+    far_in_q,
+    middle,
+    second,
+    act,
+    gpre,
+    branch,
+    stage,
+    local_sems,
+    stage_sems,
+    send_sems,
+    recv_sems,
+):
+    chunks, blocks, own, width = second.shape
+    rows = blocks * own
+    hidden = wu_ref.shape[1]
+    core, far = peers()
+
+    for j, source in enumerate((g0_ref, g1_ref, g2_ref, g3_ref)):
+        pltpu.make_async_copy(source, g_all.at[:, j], local_sems.at[j]).start()
+
+    def core_copy(step, r, source, target):
+        return remote(source.at[r], target.at[r], send_sems.at[step, r], recv_sems.at[step, r], core)
+
+    def far_copy(step, r, source, target):
+        return remote(source.at[r], target.at[r], send_sems.at[step, r], recv_sems.at[step, r], far)
+
+    def spread_core(step, r, rows_ref):
+        return remote(rows_ref.at[r, 0], rows_ref.at[r, 1], send_sems.at[step, r], recv_sems.at[step, r], core)
+
+    def spread_far(step, r, rows_ref):
+        return remote(rows_ref.at[r, 0], rows_ref.at[r, 2], send_sems.at[step, r], recv_sems.at[step, r], far)
+
+    def spread_relay(step, r, rows_ref):
+        return remote(rows_ref.at[r, 2], rows_ref.at[r, 3], send_sems.at[step, r], recv_sems.at[step, r], core)
+
+    def split(r, total, kept_ref, out_ref):
+        kept_ref[r, 0] = total[:own].astype(kept_ref.dtype)
+        out_ref[r, 0] = total[own : 2 * own].astype(LOW)
+        kept_ref[r, 1] = total[2 * own : 3 * own].astype(kept_ref.dtype)
+        out_ref[r, 1] = total[3 * own :].astype(LOW)
+
+    def fold(r, kept_ref, in_ref, out_ref):
+        out_ref[r] = (kept_ref[r, 1].astype(F32) + in_ref[r, 1].astype(F32)).astype(LOW)
+        kept_ref[r, 0] = (kept_ref[r, 0].astype(F32) + in_ref[r, 0].astype(F32)).astype(kept_ref.dtype)
+
+    def each(body):
+        lax.fori_loop(0, chunks, lambda r, carry: (body(r), carry)[1], 0)
+
+    greet((core, far))
+
+    def out_projection(r):
+        rows_here = pl.ds(pl.multiple_of(r * rows, rows), rows)
+        split(r, contract(att_ref[rows_here], wo_ref[...], 1, 0), kept, core_out)
+        core_copy(0, r, core_out, core_in).start()
+
+    each(out_projection)
+
+    def out_fold(r):
+        core_copy(0, r, core_out, core_in).wait()
+        fold(r, kept, core_in, far_out)
+        far_copy(1, r, far_out, far_in).start()
+
+    each(out_fold)
+
+    def norm(r):
+        far_copy(1, r, far_out, far_in).wait()
+        values = tok_ref[r].astype(F32) + (kept[r, 0] + far_in[r].astype(F32) + vec_ref[0:1])
+        middle[r] = values
+        second[r, 0] = (norm_parts(values)[0] * vec_ref[1:2] + vec_ref[2:3]).astype(LOW)
+        spread_core(2, r, second).start()
+        spread_far(3, r, second).start()
+
+    each(norm)
+    for j, source in enumerate((g0_ref, g1_ref, g2_ref, g3_ref)):
+        pltpu.make_async_copy(source, g_all.at[:, j], local_sems.at[j]).wait()
+
+    sum_up_ref[...] = jnp.zeros_like(sum_up_ref)
+
+    def feed(r):
+        spread_far(3, r, second).wait()
+        spread_relay(4, r, second).start()
+        spread_core(2, r, second).wait()
+        spread_relay(4, r, second).wait()
+        pre = contract(second[r].reshape(rows, width), wu_ref[...], 1, 0) + bias_up_ref[...]
+        activated, slope = gelu_parts(pre)
+        act[r] = activated.astype(LOW).reshape(blocks, own, hidden)
+        grads = contract(g_all[r].reshape(rows, width), wd_ref[...], 1, 1) * slope
+        grads_low = grads.astype(LOW)
+        gpre[r] = grads_low.reshape(blocks, own, hidden)
+        sum_up_ref[...] += jnp.sum(grads_low.astype(F32), axis=0, keepdims=True)
+        split(r, contract(grads_low, wu_ref[...], 1, 1), kept, core_out)
+        core_copy(5, r, core_out, core_in).start()
+        core_copy(5, r, core_out, core_in).wait()
+        fold(r, kept, core_in, far_out)
+        far_copy(6, r, far_out, far_in).start()
+        split(r, contract(act[r].reshape(rows, hidden), wd_ref[...], 1, 0), kept_q, core_out)
+        core_copy(7, r, core_out, core_in_q).start()
+
+    each(feed)
+    sums_ref[...] = jnp.zeros_like(sums_ref)
+
+    def norm_grad(r):
+        far_copy(6, r, far_out, far_in).wait()
+        grads = kept[r, 0] + far_in[r].astype(F32)
+        unit, scale = norm_parts(middle[r])
+        place = g_all[r, 0].astype(F32)
+        total = place + norm_back(grads, vec_ref[1:2], unit, scale)
+        gmid_ref[r] = total
+        low = total.astype(LOW)
+        branch[r, 0] = low
+        spread_core(9, r, branch).start()
+        spread_far(10, r, branch).start()
+        sums_ref[0:1] += jnp.sum(low.astype(F32), axis=0, keepdims=True)
+        sums_ref[1:2] += jnp.sum(grads * unit, axis=0, keepdims=True)
+        sums_ref[2:3] += jnp.sum(grads, axis=0, keepdims=True)
+        sums_ref[3:4] += jnp.sum(place, axis=0, keepdims=True)
+
+    each(norm_grad)
+
+    def result_fold(r):
+        core_copy(7, r, core_out, core_in_q).wait()
+        fold(r, kept_q, core_in_q, far_out_q)
+        far_copy(8, r, far_out_q, far_in_q).start()
+
+    each(result_fold)
+
+    wide = 256
+    flat_second = second.reshape(chunks * rows, width)
+    flat_act = act.reshape(chunks * rows, hidden)
+    flat_gpre = gpre.reshape(chunks * rows, hidden)
+    flat_g = g_all.reshape(chunks * rows, width)
+    flat_branch = branch.reshape(chunks * rows, width)
+
+    def down_grad(t):
+        part = pl.ds(pl.multiple_of(t * wide, wide), wide)
+        total = contract(flat_act[:, part], flat_g[...], 0, 0).astype(LOW)
+        for b in range(8):
+            stage[b] = total[:, b * own : (b + 1) * own]
+        copy = pltpu.make_async_copy(stage, gdown_ref.at[:, part], stage_sems.at[0])
+        copy.start()
+        copy.wait()
+
+    lax.fori_loop(0, hidden // wide, lambda t, c: (down_grad(t), c)[1], 0)
+
+    def attended_grad(r):
+        spread_far(10, r, branch).wait()
+        spread_relay(11, r, branch).start()
+        spread_core(9, r, branch).wait()
+        spread_relay(11, r, branch).wait()
+        rows_here = pl.ds(pl.multiple_of(r * rows, rows), rows)
+        gatt_ref[rows_here] = contract(branch[r].reshape(rows, width), wo_ref[...], 1, 1).astype(LOW)
+
+    each(attended_grad)
+
+    def up_grad(t):
+        part = pl.ds(pl.multiple_of(t * wide, wide), wide)
+        total = contract(flat_second[:, part], flat_gpre[...], 0, 0).astype(LOW)
+        for b in range(2):
+            gup_ref[2 * t + b] = total[b * own : (b + 1) * own]
+
+    lax.fori_loop(0, width // wide, lambda t, c: (up_grad(t), c)[1], 0)
+    total_out = contract(att_ref[...], flat_branch[...], 0, 0).astype(LOW)
+    for b in range(8):
+        gout_ref[b] = total_out[:, b * own : (b + 1) * own]
+
+    def finish(r):
+        far_copy(8, r, far_out_q, far_in_q).wait()
+        total = kept_q[r, 0].astype(F32) + far_in_q[r].astype(F32)
+        result_ref[r] = (middle[r] + (total + vec_ref[3:4])).astype(LOW)
+
+    each(finish)
+
+
+def feed_block(attended, w_output, w_up, w_down, own_tokens, grads, vectors, bias_up):
+    chunks, own, width = own_tokens.shape
+    rows = chunks * 4 * own
+    head_width = w_output.shape[0]
+    hidden = w_up.shape[1]
+    half = (chunks, 2, own, width)
+    one = (chunks, own, width)
+    all_rows = (chunks, 4, own, width)
+    vmem = pl.BlockSpec(memory_space=pltpu.VMEM)
+    hbm = pl.BlockSpec(memory_space=pl.ANY)
+    return pl.pallas_call(
+        feed_kernel,
+        in_specs=[vmem] * 5 + [hbm] * 4 + [vmem] * 2,
+        out_specs=[vmem] * 5 + [hbm] + [vmem] * 2,
+        out_shape=[
+            jax.ShapeDtypeStruct(one, LOW),
+            jax.ShapeDtypeStruct((rows, head_width), LOW),
+            jax.ShapeDtypeStruct(one, F32),
+            jax.ShapeDtypeStruct((8, head_width, width // 8), LOW),
+            jax.ShapeDtypeStruct((8, width // 8, hidden), LOW),
+            jax.ShapeDtypeStruct((8, hidden, width // 8), LOW),
+            jax.ShapeDtypeStruct((8, width), F32),
+            jax.ShapeDtypeStruct((1, hidden), F32),
+        ],
+        scratch_shapes=[
+            pltpu.VMEM(all_rows, LOW),
+            pltpu.VMEM(half, F32),
+            pltpu.VMEM(half, LOW),
+            pltpu.VMEM(half, LOW),
+            pltpu.VMEM(half, LOW),
+            pltpu.VMEM(half, LOW),
+            pltpu.VMEM(one, LOW),
+            pltpu.VMEM(one, LOW),
+            pltpu.VMEM(one, LOW),
+            pltpu.VMEM(one, LOW),
+            pltpu.VMEM(one, F32),
+            pltpu.VMEM(all_rows, LOW),
+            pltpu.VMEM((chunks, 4, own, hidden), LOW),
+            pltpu.VMEM((chunks, 4, own, hidden), LOW),
+            pltpu.VMEM(all_rows, LOW),
+            pltpu.VMEM((8, 256, width // 8), LOW),
+            pltpu.SemaphoreType.DMA((4,)),
+            pltpu.SemaphoreType.DMA((2,)),
+            pltpu.SemaphoreType.DMA((12, chunks)),
+            pltpu.SemaphoreType.DMA((12, chunks)),
+        ],
+        compiler_params=pltpu.CompilerParams(
+            collective_id=1, has_side_effects=True, vmem_limit_bytes=61 * 1024 * 1024
+        ),
+        cost_estimate=pl.CostEstimate(flops=100_000_000_000, bytes_accessed=30_000_000, transcendentals=0),
+        name="feed_block",
+    )(attended, w_output, w_up, w_down, own_tokens, *grads, vectors, bias_up)
 
 
 def local_sequence(
@@ -647,7 +942,7 @@
     inputs = inputs_low.astype(F32)
     grad_result = trade_rows(cotangent).astype(F32) * validity
     tokens_all = gather_rows(inputs_low).reshape(seq_rows, width).astype(F32)
-    grad_result_all = gather_rows(grad_result.astype(LOW)).reshape(seq_rows, width)
+    grad_all = gather_parts(grad_result.astype(LOW))
 
     normed_all = (norm_parts(tokens_all)[0] * first_gain + first_shift).astype(LOW)
     projected = product(normed_all, query_key_value)
@@ -659,27 +954,13 @@
     def split_rows(array):
         return array.reshape(micro_count, col_count, own_rows, -1)
 
-    branch = scatter_rows(split_rows(product(attended, output_full))) + bias_output
-    middle = inputs + branch
-    unit, scale = norm_parts(middle)
-    second_normed = (unit * second_gain + second_shift).astype(LOW)
-    second_all = gather_rows(second_normed).reshape(seq_rows, width)
-    pre_activation = product(second_all, up_full) + bias_up
-    activated = gelu_tanh(pre_activation).astype(LOW)
-    result = middle + scatter_rows(split_rows(product(activated, down_full))) + bias_down
-    result = trade_rows(result.astype(LOW))
-
-    grad_down = transposed_left(activated, grad_result_all)
-    grad_activated = transposed_right(grad_result_all, down_full)
-    gelu_back = jax.vjp(gelu_tanh, pre_activation)[1]
-    grad_pre = gelu_back(grad_activated)[0].astype(LOW)
-    grad_up = transposed_left(second_all, grad_pre)
-    grad_second = scatter_rows(split_rows(transposed_right(grad_pre, up_full)))
-    grad_middle = grad_result + norm_back(grad_second, second_gain, unit, scale)
-    grad_branch = grad_middle.astype(LOW)
-    grad_branch_all = gather_rows(grad_branch).reshape(seq_rows, width)
-    grad_output = transposed_left(attended, grad_branch_all)
-    grad_attended = transposed_right(grad_branch_all, output_full).astype(LOW)
+    vectors = jnp.concatenate(
+        [jnp.stack([bias_output, second_gain, second_shift, bias_down]), jnp.zeros((4, width), F32)]
+    )
+    result, grad_attended, grad_middle, grad_output, grad_up, grad_down, sums, sum_up = feed_block(
+        attended, output_full, up_full, down_full, inputs_low, grad_all, vectors, bias_up.reshape(1, -1)
+    )
+    result = trade_rows(result)
     grad_queries, grad_keys, grad_values = attention_back(
         queries, keys, values, grad_attended, attended, lse, key_bias, causal
     )
@@ -691,8 +972,9 @@
     grad_tokens = trade_rows(grad_tokens.astype(LOW))
 
     grad_w = scatter_blocks(grad_w, 0)
-    grad_trailing = scatter_blocks(jnp.concatenate([grad_output, grad_down], axis=0), 1)
-    grad_up = scatter_blocks(grad_up, 0)
+    grad_output = scatter_blocks(grad_output, 0)[0]
+    grad_down = scatter_blocks(grad_down, 0)[0]
+    grad_up = scatter_blocks(grad_up, 0)[0]
 
     def over_rows(array):
         return jnp.sum(array.astype(F32).reshape(-1, array.shape[-1]), axis=0)
@@ -702,16 +984,16 @@
             [
                 over_rows(grad_first * first_unit),
                 over_rows(grad_first),
-                over_rows(grad_branch),
-                over_rows(grad_second * unit),
-                over_rows(grad_second),
-                over_rows(grad_result),
+                sums[0],
+                sums[1],
+                sums[2],
+                sums[3],
             ]
         ),
         ("dp", "row", "col"),
     )
     by_col = lax.psum(
-        jnp.concatenate([over_rows(grad_queries), over_rows(grad_values), over_rows(grad_pre)]), ("dp", "row")
+        jnp.concatenate([over_rows(grad_queries), over_rows(grad_values), sum_up[0]]), ("dp", "row")
     )
     return (
         result,
@@ -723,13 +1005,13 @@
         grad_w[:, 2 * head_width :],
         by_col[:head_width],
         by_col[head_width : 2 * head_width],
-        grad_trailing[:head_width],
+        grad_output,
         shared[2],
         shared[3],
         shared[4],
         grad_up,
         by_col[2 * head_width :],
-        grad_trailing[head_width:],
+        grad_down,
         shared[5],
     )
 

time: 644 us -> 575 us (0.89)
  waiting for transfers between devices: 282 us -> 155 us
  Pallas kernels: 59.7 us -> 186 us
  matrix products: 69.9 us -> 12.6 us
  blocking collectives: 59.7 us -> 101 us
  other arithmetic: 63.4 us -> 37.8 us
  local copies, waits for them, and re-layouts: 52.8 us -> 31.1 us
    pallas_call x0 -> x1, Pallas kernels: none -> 127 us  [feed_block(): pl.pallas_call(feed_kernel, in_specs=[vmem] * 5 + [hbm] * 4 + [vmem] * 2,...]
    ppermute x29 -> x20, waiting for transfers between devices: 221 us -> 110 us  [swap(): lax.ppermute(array, axis, [(place, place ^ flip) for place in range(size)])]
    all_to_all x0 -> x1, blocking collectives: none -> 40.4 us  [trade_rows(): return lax.all_to_all(array, 'row', split_axis=0, concat_axis=0)]
    all_to_all x4 -> x3, waiting for transfers between devices: 52.7 us -> 29.2 us  [trade_rows(): return lax.all_to_all(array, 'row', split_axis=0, concat_axis=0)]
    dot_general x4 -> x1, matrix products: 24.6 us -> 3.46 us  [transposed_right(): lax.dot_general(former, latter, (((1,), (1,)), ((), ())), preferred_eleme...]
    dot_general x4 -> x1, matrix products: 24.1 us -> 3.51 us  [transposed_left(): lax.dot_general(former, latter, (((0,), (0,)), ((), ())), preferred_eleme...]
    all_gather x1, waiting for transfers between devices: 0.01 us -> 16.4 us  [local_sequence(): up_full = lax.all_gather(w_up, ('dp', 'row'), axis=0, tiled=True)]
    dot_general x4 -> x1, matrix products: 21.2 us -> 5.67 us  [product(): return jnp.dot(former, latter, preferred_element_type=jnp.float32)]
  transfers between devices with their start and end apart: 36 -> 26, of which waited for: 17 -> 12; matrix products, arithmetic and copies ran while one was open for 23% -> 11% of each run, Pallas kernels for 9% -> 4%
where the time goes in v2:
time: 575 us; the launch traced here: 568 us
  Pallas kernels  186 us (32%)
  waiting for transfers between devices  155 us (27%)
  blocking collectives  101 us (18%)
  other arithmetic  37.8 us (7%)
  local copies, waits for them, and re-layouts  31.1 us (5%)
  starting transfers between devices  29.5 us (5%)
  between operations  15 us (3%)
  matrix products  12.6 us (2%)
    pallas_call x1, Pallas kernels, feed_block(): pl.pallas_call(feed_kernel, in_specs=[vmem] * 5 + [hbm] * 4 + [vmem] * 2,...  127 us
    ppermute x20, waiting for transfers between devices, swap(): lax.ppermute(array, axis, [(place, place ^ flip) for place in range(size)])  110 us
    all_to_all x1, blocking collectives, trade_rows(): return lax.all_to_all(array, 'row', split_axis=0, concat_axis=0)  40.4 us
    psum x1, blocking collectives, local_sequence(): lax.psum(jnp.stack([over_rows(grad_first * first_unit), over_rows(grad_fi...  39.6 us
    pallas_call x1, Pallas kernels, attention_back(): pl.pallas_call(attention_back_kernel, grid=(pairs, chunks), in_specs=[row...  34.7 us
    all_to_all x3, waiting for transfers between devices, trade_rows(): return lax.all_to_all(array, 'row', split_axis=0, concat_axis=0)  29.2 us
    pallas_call x1, Pallas kernels, attention_out(): pl.pallas_call(attention_out_kernel, grid=(pairs, chunks), in_specs=[row_...  24.4 us
    psum x1, blocking collectives, local_sequence(): lax.psum(jnp.concatenate([over_rows(grad_queries), over_rows(grad_values)...  20.6 us
  transfers between devices with their start and end apart: 26, of which 12 were waited for; matrix products, arithmetic and copies ran while one was open for 11% of the time, Pallas kernels for 4%

profile of v2, /device:TPU:0, one launch (start us, length us, event | category | flops | bytes accessed | tf_op | source)
XLA Modules:
  0.0 568.2 jit_solution(5152120822564658489)
XLA Ops:
  7.3 1.6 pad_maximum_fusion.1
  8.9 1.7 pad_maximum_fusion
  10.6 40.4 %all_to_all.20.tok_ref = bf16[4,128,1024]{2,1,0:T(8,128)(2,1)S(1)} all-to-all(bf16[4,128,1024]{2,1,0:T(8,128)(2,1)} %param.18), channel_id=1, replica_groups=mesh['dp'=2,'row'=4,'col'=4] {'row'}, dimensions={0} | all-to-all | bytes 2097152 | tf_op jit(solution)/shard_map/all_to_all | solution.py:575
  51.1 4.6 all-to-all-start.1
  55.7 1.6 collective-permute-start.1
  58.7 29.2 %all-to-all-done.1 = bf16[4,128,1024]{2,1,0:T(8,128)(2,1)} async-done(((bf16[4,128,1024]{2,1,0:T(8,128)(2,1)}), bf16[4,128,1024]{2,1,0:T(8,128)(2,1)}, u32[]{:S(2)}, u32[]{:S(2)}) %all-to-all-start.1) | async-done | bytes 1048608 | tf_op jit(solution)/shard_map/all_to_all | solution.py:575
  89.4 1.6 collective-permute-start.4
  94.4 1.5 compare_select_fusion
  97.1 15.3 %collective-permute-done.4.g2_ref = bf16[4,128,1024]{2,1,0:T(8,128)(2,1)} collective-permute-done((bf16[4,128,1024]{2,1,0:T(8,128)(2,1)S(1)}, bf16[4,128,1024]{2,1,0:T(8,128)(2,1)}, u32[]{:S(2)}, u32[]{:S(2)}) %collective-permute-start.4) | collective-permute-done | bytes 1048608 | tf_op jit(solution)/shard_map/ppermute | solution.py:555
  112.4 1.9 fusion.22
  114.3 2.6 multiply_reduce_fusion
  117.0 1.9 maximum_convert_fusion
  119.0 1.7 copy.40
  120.7 3.4 fusion.3
  124.0 5.7 fusion.27
  130.9 1.8 fusion.17
  132.6 24.4 %attention_out.1 = (bf16[2048,256]{1,0:T(8,128)(2,1)}, f32[2,4,2,512]{3,2,1,0:T(2,128)}) custom-call(bf16[2048,256]{1,0:T(8,128)(2,1)} %get-tuple-element.50.q_ref, bf16[2048,256]{1,0:T(8,128)(2,1)} %slice.141.k_ref, bf16[2048,256]{1,0:T(8,128)(2,1)} %get-tuple-element.49.v_ref, f32[1,2048]{1,0:T(1,128)} %bitcast.81, f32[512,512]{1,0:T(8,128)} %get-tuple-element.63.causal_ref), custom_call_target="tpu_custom_call" | custom-call | flops 40000000000 | bytes 4000000 | tf_op jit(solution)/shard_map/attention_out/pallas_call | solution.py:460
  157.0 3.1 slice.102.wd_ref
  160.1 1.9 slice.101.wo_ref
  162.0 16.4 %all-gather.8.cloned.1.call-done.wu_ref = bf16[1024,1024]{1,0:T(8,128)(2,1)} async-done(((bf16[128,1024]{1,0:T(8,128)(2,1)}), bf16[1024,1024]{1,0:T(8,128)(2,1)}) %all-gather.8.cloned.1.call-update) | async-done | bytes 2097168 | tf_op jit(solution)/shard_map/all_gather | solution.py:939
  178.4 127.2 %feed_block.1 = (bf16[4,128,1024]{2,1,0:T(8,128)(2,1)}, bf16[2048,256]{1,0:T(8,128)(2,1)}, f32[4,128,1024]{2,1,0:T(8,128)}, bf16[8,256,128]{2,1,0:T(8,128)(2,1)}...) custom-call(bf16[2048,256]{1,0:T(8,128)(2,1)} %get-tuple-element.30.att_, ...), custom_call_target="tpu_custom_call" | custom-call | flops 99999997952 | bytes 30000000 | tf_op jit(solution)/shard_map/feed_block/pallas_call | solution.py:850
  305.6 34.7 %attention_back.1 = (bf16[2048,256]{1,0:T(8,128)(2,1)}, bf16[2048,256]{1,0:T(8,128)(2,1)}, bf16[2048,256]{1,0:T(8,128)(2,1)}) custom-call(bf16[2048,256]{1,0:T(8,128)(2,1)} %get-tuple-element.50.q_ref, bf16[2048,256]{1,0:T(8,128)(2,1)} %slice.141.k_ref, bf16[2048,256]{1,0:T(8,128)(2,1)} %get-tuple-element.49.v_ref, ...), custom_call_target="tpu_custom_call" | custom-call | flops 80000000000 | bytes 6000000 | tf_op jit(solution)/shard_map/attention_back/pallas_call | solution.py:531
  343.2 3.5 fusion.28
  346.6 3.3 fusion.23
  349.9 2.2 copy.47
  355.1 1.5 collective-permute-start.11
  356.8 3.5 fusion.29
  362.3 20.6 %psum.15 = f32[1536]{0:T(1024)S(1)} all-reduce(f32[1536]{0:T(1024)S(1)} %pad_maximum_fusion.3), channel_id=1, replica_groups=mesh['dp'=2,'row'=4,'col'=4] {'dp','row'}, use_global_device_ids=true, to_apply=%region_11.12 | all-reduce | flops 1536 | bytes 12288 | tf_op jit(solution)/shard_map/psum | solution.py:995
  383.0 3.3 collective-permute-done.11
  388.6 5.9 %collective-permute-done.12 = bf16[2,256,128]{2,1,0:T(8,128)(2,1)S(1)} collective-permute-done((bf16[2,256,128]{2,1,0:T(8,128)(2,1)S(1)}, bf16[2,256,128]{2,1,0:T(8,128)(2,1)S(1)}, u32[]{:S(2)}, u32[]{:S(2)}) %collective-permute-start.12) | collective-permute-done | bytes 131104 | tf_op jit(solution)/shard_map/ppermute | solution.py:555
  396.6 3.8 all-to-all-start.2
  401.1 2.2 collective-permute-done.8
  403.2 1.8 convert_add_fusion.2
  408.0 1.7 collective-permute-start.18
  409.7 45.1 %collective-permute-done.9 = bf16[256,768]{1,0:T(8,128)(2,1)S(1)} collective-permute-done((bf16[256,768]{1,0:T(8,128)(2,1)S(1)}, bf16[256,768]{1,0:T(8,128)(2,1)S(1)}, u32[]{:S(2)}, u32[]{:S(2)}) %collective-permute-start.9) | collective-permute-done | bytes 393248 | tf_op jit(solution)/shard_map/ppermute | solution.py:555
  454.9 3.3 copy_add_fusion
  459.2 1.6 convert_add_fusion.1
  461.6 2.8 collective-permute-start.15
  464.4 4.9 collective-permute-done.10
  469.3 8.0 %collective-permute-done.18 = bf16[2,1024,128]{2,1,0:T(8,128)(2,1)S(1)} collective-permute-done((bf16[2,1024,128]{2,1,0:T(8,128)(2,1)S(1)}, bf16[2,1024,128]{2,1,0:T(8,128)(2,1)S(1)}, u32[]{:S(2)}, u32[]{:S(2)}) %collective-permute-start.18) | collective-permute-done | bytes 524320 | tf_op jit(solution)/shard_map/ppermute | solution.py:555
  478.4 3.2 collective-permute-done.7
  482.8 1.9 fusion.13
  484.7 4.3 all-to-all-start.3
  490.1 2.0 collective-permute-start.19
  494.3 19.1 %collective-permute-done.19 = bf16[1,1024,128]{2,1,0:T(8,128)(2,1)S(1)} collective-permute-done((bf16[1,1024,128]{2,1,0:T(8,128)(2,1)S(1)}, bf16[1,1024,128]{2,1,0:T(8,128)(2,1)S(1)}, u32[]{:S(2)}, u32[]{:S(2)}) %collective-permute-start.19) | collective-permute-done | bytes 262176 | tf_op jit(solution)/shard_map/ppermute | solution.py:555
  514.2 2.8 collective-permute-done.16
  517.8 39.6 %psum.14 = f32[6,1024]{1,0:T(8,128)S(1)} all-reduce(f32[6,1024]{1,0:T(8,128)S(1)} %pad_maximum_fusion.2), channel_id=1, replica_groups=mesh['dp'=2,'row'=4,'col'=4] {'dp','row','col'}, use_global_device_ids=true, to_apply=%region_8.9 | all-reduce | flops 6144 | bytes 49152 | tf_op jit(solution)/shard_map/psum | solution.py:982
  559.0 2.3 copy.57
  (167 shorter events, 35.4 us)
Async XLA Ops:
  7.2 50.2 %copy-start = (s32[1,4]{1,0:T(1,128)S(1)}, s32[1,4]{1,0:T(1,128)}, u32[]{:S(2)}) copy-start(s32[1,4]{1,0:T(1,128)} %param.19) | copy-start | bytes 52
  7.2 116.8 %all-gather.4.cloned.1.call-start = ((), (), s32[]{:S(2)}) async-start(), calls=%async_computation.4 | async-start | bytes 1769472 | tf_op jit(solution)/shard_map/all_gather | solution.py:934
  8.9 148.1 %all-gather.6.cloned.1.call-start = ((), (), s32[]{:S(2)}) async-start(), calls=%async_computation.5 | async-start | bytes 2949120 | tf_op jit(solution)/shard_map/all_gather | solution.py:937
  51.1 65.9 %copy-start.2 = (bf16[4,128,1024]{2,1,0:T(8,128)(2,1)}, bf16[4,128,1024]{2,1,0:T(8,128)(2,1)S(1)}, u32[]{:S(2)}) copy-start(bf16[4,128,1024]{2,1,0:T(8,128)(2,1)S(1)} %all_to_all.20.tok_ref) | copy-start | bytes 3145732
  51.1 42.6 %copy-start.28 = (f32[1024]{0:T(1024)S(1)}, f32[1024]{0:T(1024)}, u32[]{:S(2)}) copy-start(f32[1024]{0:T(1024)} %param.28) | copy-start | bytes 12292
  51.1 42.6 %copy-start.29 = (f32[1024]{0:T(1024)S(1)}, f32[1024]{0:T(1024)}, u32[]{:S(2)}) copy-start(f32[1024]{0:T(1024)} %param.29) | copy-start | bytes 12292
  51.1 42.6 %copy-start.30 = (f32[1024]{0:T(1024)S(1)}, f32[1024]{0:T(1024)}, u32[]{:S(2)}) copy-start(f32[1024]{0:T(1024)} %param.30) | copy-start | bytes 12292
  51.1 42.6 %copy-start.31 = (f32[1024]{0:T(1024)S(1)}, f32[1024]{0:T(1024)}, u32[]{:S(2)}) copy-start(f32[1024]{0:T(1024)} %param.34) | copy-start | bytes 12292
  51.1 36.9 %all-to-all-start.1 = ((bf16[4,128,1024]{2,1,0:T(8,128)(2,1)}), bf16[4,128,1024]{2,1,0:T(8,128)(2,1)}, u32[]{:S(2)}, u32[]{:S(2)}) async-start(bf16[4,128,1024]{2,1,0:T(8,128)(2,1)} %param.35), calls=%async_computation.1 | async-start | bytes 2097152 | tf_op jit(solution)/shard_map/all_to_all | solution.py:575
  55.7 122.7 %all-gather.8.cloned.1.call-start = ((), (), s32[]{:S(2)}) async-start(), calls=%async_computation.6 | async-start | bytes 2359296 | tf_op jit(solution)/shard_map/all_gather | solution.py:939
  55.7 35.4 %collective-permute-start.1 = (bf16[4,128,1024]{2,1,0:T(8,128)(2,1)S(1)}, bf16[4,128,1024]{2,1,0:T(8,128)(2,1)S(1)}, u32[]{:S(2)}, u32[]{:S(2)}) collective-permute-start(bf16[4,128,1024]{2,1,0:T(8,128)(2,1)S(1)} %all_to_all.20.tok_ref), channel_id=1, source_target_pairs={{0,2},{1,3},{2,0},{3,1},{4,6},{5,7},{6,4},{7,5},{8,10},{9,11},{10,... | collective-permute-start | bytes 3145736 | tf_op jit(solution)/shard_map/ppermute | solution.py:555
  89.4 24.9 %copy-start.17 = (bf16[4,128,1024]{2,1,0:T(8,128)(2,1)}, bf16[4,128,1024]{2,1,0:T(8,128)(2,1)S(1)}, u32[]{:S(2)}) copy-start(bf16[4,128,1024]{2,1,0:T(8,128)(2,1)S(1)} %multiply_convert_fusion.g0_ref) | copy-start | bytes 3145732
  89.4 23.0 %collective-permute-start.4 = (bf16[4,128,1024]{2,1,0:T(8,128)(2,1)S(1)}, bf16[4,128,1024]{2,1,0:T(8,128)(2,1)}, u32[]{:S(2)}, u32[]{:S(2)}) collective-permute-start(bf16[4,128,1024]{2,1,0:T(8,128)(2,1)S(1)} %multiply_convert_fusion.g0_ref), channel_id=1, source_target_pairs={{0,2},{1,3},{2,0},{3,1},{4,6},{5,7},{6,4},{7,5},{8,10},{9,11},{10,... | collective-permute-start | bytes 3145736 | tf_op jit(solution)/shard_map/ppermute | solution.py:555
  91.0 21.3 %collective-permute-start = (bf16[4,128,1024]{2,1,0:T(8,128)(2,1)S(1)}, bf16[4,128,1024]{2,1,0:T(8,128)(2,1)}, u32[]{:S(2)}, u32[]{:S(2)}) collective-permute-start(bf16[4,128,1024]{2,1,0:T(8,128)(2,1)S(1)} %all_to_all.20.tok_ref), channel_id=1, source_target_pairs={{0,1},{1,0},{2,3},{3,2},{4,5},{5,4},{6,7},{7,6},{8,9},{9,8},{10,11... | collective-permute-start | bytes 3145736 | tf_op jit(solution)/shard_map/ppermute | solution.py:555
  91.1 21.3 %collective-permute-start.2 = (bf16[4,128,1024]{2,1,0:T(8,128)(2,1)S(1)}, bf16[4,128,1024]{2,1,0:T(8,128)(2,1)}, u32[]{:S(2)}, u32[]{:S(2)}) collective-permute-start(bf16[4,128,1024]{2,1,0:T(8,128)(2,1)S(1)} %collective-permute-done.1), channel_id=1, source_target_pairs={{0,1},{1,0},{2,3},{3,2},{4,5},{5,4},{6,7},{7,6},{8,9},{9,8},{10,11... | collective-permute-start | bytes 3145736 | tf_op jit(solution)/shard_map/ppermute | solution.py:555
  92.3 22.0 %copy-start.22 = (f32[1,1,4,512]{3,1,2,0:T(1,128)}, f32[1,1,4,512]{3,1,2,0:T(1,128)S(1)}, u32[]{:S(2)}) copy-start(f32[1,1,4,512]{3,1,2,0:T(1,128)S(1)} %copy.48) | copy-start | bytes 24580
  95.9 66.1 %collective-permute-start.3 = (bf16[4,128,1024]{2,1,0:T(8,128)(2,1)S(1)}, bf16[4,128,1024]{2,1,0:T(8,128)(2,1)}, u32[]{:S(2)}, u32[]{:S(2)}) collective-permute-start(bf16[4,128,1024]{2,1,0:T(8,128)(2,1)S(1)} %multiply_convert_fusion.g0_ref), channel_id=1, source_target_pairs={{0,1},{1,0},{2,3},{3,2},{4,5},{5,4},{6,7},{7,6},{8,9},{9,8},{10,11... | collective-permute-start | bytes 3145736 | tf_op jit(solution)/shard_map/ppermute | solution.py:555
  96.1 20.8 %copy-start.23 = (f32[4,128]{1,0:T(4,128)}, f32[4,128]{1,0:T(4,128)S(1)}, u32[]{:S(2)}) copy-start(f32[4,128]{1,0:T(4,128)S(1)} %broadcast_multiply_fusion.3) | copy-start | bytes 6148
  112.4 49.6 %collective-permute-start.5 = (bf16[4,128,1024]{2,1,0:T(8,128)(2,1)}, bf16[4,128,1024]{2,1,0:T(8,128)(2,1)}, u32[]{:S(2)}, u32[]{:S(2)}) collective-permute-start(bf16[4,128,1024]{2,1,0:T(8,128)(2,1)} %collective-permute-done.4.g2_ref), channel_id=1, source_target_pairs={{0,1},{1,0},{2,3},{3,2},{4,5},{5,4},{6,7},{7,6},{8,9},{9,8},{10,11... | collective-permute-start | bytes 3145736 | tf_op jit(solution)/shard_map/ppermute | solution.py:555
  124.0 6.8 %copy-start.33 = (f32[256]{0:T(256)S(1)}, f32[256]{0:T(256)}, u32[]{:S(2)}) copy-start(f32[256]{0:T(256)} %param.26) | copy-start | bytes 3076
  124.0 6.8 %copy-start.34 = (f32[256]{0:T(256)S(1)}, f32[256]{0:T(256)}, u32[]{:S(2)}) copy-start(f32[256]{0:T(256)} %param.25) | copy-start | bytes 3076
  352.2 102.7 %collective-permute-start.6 = (f32[4,2,128,1024]{3,2,0,1:T(8,128)}, f32[4,2,128,1024]{3,2,0,1:T(8,128)}, u32[]{:S(2)}, u32[]{:S(2)}) collective-permute-start(f32[4,2,128,1024]{3,2,0,1:T(8,128)} %copy.47), channel_id=1, source_target_pairs={{0,1},{1,0},{2,3},{3,2},{4,5},{5,4},{6,7},{7,6},{8,9},{9,8},{10,11... | collective-permute-start | bytes 12582920 | tf_op jit(solution)/shard_map/ppermute | solution.py:555
  352.6 7.7 %copy-start.5 = (f32[8,1024,128]{2,1,0:T(8,128)}, f32[8,1024,128]{2,1,0:T(8,128)S(1)}, u32[]{:S(2)}) copy-start(f32[8,1024,128]{2,1,0:T(8,128)S(1)} %convert_element_type.172) | copy-start | bytes 12582916
  353.7 52.7 %collective-permute-start.17 = (bf16[4,1024,128]{2,1,0:T(8,128)(2,1)}, bf16[4,1024,128]{2,1,0:T(8,128)(2,1)}, u32[]{:S(2)}, u32[]{:S(2)}) collective-permute-start(bf16[4,1024,128]{2,1,0:T(8,128)(2,1)} %dynamic-slice_convert_fusion), channel_id=1, source_target_pairs={{0,16},{16,0},{1,17},{17,1},{2,18},{18,2},{3,19},{19,3},{4,20},{20... | collective-permute-start | bytes 3145736 | tf_op jit(solution)/shard_map/ppermute | solution.py:555
  355.1 31.1 %collective-permute-start.11 = (bf16[4,256,128]{2,1,0:T(8,128)(2,1)}, bf16[4,256,128]{2,1,0:T(8,128)(2,1)S(1)}, u32[]{:S(2)}, u32[]{:S(2)}) collective-permute-start(bf16[4,256,128]{2,1,0:T(8,128)(2,1)} %dynamic-slice_convert_fusion.8), channel_id=1, source_target_pairs={{0,16},{16,0},{1,17},{17,1},{2,18},{18,2},{3,19},{19,3},{4,20},{20... | collective-permute-start | bytes 786440 | tf_op jit(solution)/shard_map/ppermute | solution.py:555
  360.3 27.8 %copy-start.13 = (bf16[8,128,1024]{2,1,0:T(8,128)(2,1)S(1)}, bf16[8,128,1024]{2,1,0:T(8,128)(2,1)}, u32[]{:S(2)}) copy-start(bf16[8,128,1024]{2,1,0:T(8,128)(2,1)} %get-tuple-element.41) | copy-start | bytes 6291460
  361.3 41.9 %collective-permute-start.8 = (bf16[512,768]{1,0:T(8,128)(2,1)}, bf16[512,768]{1,0:T(8,128)(2,1)}, u32[]{:S(2)}, u32[]{:S(2)}) collective-permute-start(bf16[512,768]{1,0:T(8,128)(2,1)} %dynamic-slice_convert_fusion.2), channel_id=1, source_target_pairs={{0,16},{16,0},{1,17},{17,1},{2,18},{18,2},{3,19},{19,3},{4,20},{20... | collective-permute-start | bytes 2359304 | tf_op jit(solution)/shard_map/ppermute | solution.py:555
  386.4 8.2 %collective-permute-start.12 = (bf16[2,256,128]{2,1,0:T(8,128)(2,1)S(1)}, bf16[2,256,128]{2,1,0:T(8,128)(2,1)S(1)}, u32[]{:S(2)}, u32[]{:S(2)}) collective-permute-start(bf16[2,256,128]{2,1,0:T(8,128)(2,1)S(1)} %dynamic-slice_convert_fusion.10), channel_id=1, source_target_pairs={{0,8},{4,12},{8,0},{12,4},{1,9},{5,13},{9,1},{13,5},{2,10},{6,14},... | collective-permute-start | bytes 393224 | tf_op jit(solution)/shard_map/ppermute | solution.py:555
  388.1 7.9 %copy-start.26 = (f32[8,1024]{1,0:T(8,128)S(1)}, f32[8,1024]{1,0:T(8,128)}, u32[]{:S(2)}) copy-start(f32[8,1024]{1,0:T(8,128)} %get-tuple-element.38) | copy-start | bytes 98308
  394.6 5.8 %collective-permute-start.13 = (bf16[1,256,128]{2,1,0:T(8,128)(2,1)S(1)}, bf16[1,256,128]{2,1,0:T(8,128)(2,1)S(1)}, u32[]{:S(2)}, u32[]{:S(2)}) collective-permute-start(bf16[1,256,128]{2,1,0:T(8,128)(2,1)S(1)} %dynamic-slice_convert_fusion.11), channel_id=1, source_target_pairs={{0,4},{4,0},{8,12},{12,8},{1,5},{5,1},{9,13},{13,9},{2,6},{6,2},{1... | collective-permute-start | bytes 196616 | tf_op jit(solution)/shard_map/ppermute | solution.py:555
  395.4 63.7 %collective-permute-start.14 = (bf16[4,128,1024]{2,1,0:T(8,128)(2,1)S(1)}, bf16[4,128,1024]{2,1,0:T(8,128)(2,1)}, u32[]{:S(2)}, u32[]{:S(2)}) collective-permute-start(bf16[4,128,1024]{2,1,0:T(8,128)(2,1)S(1)} %dynamic-slice_convert_fusion.1), channel_id=1, source_target_pairs={{0,16},{16,0},{1,17},{17,1},{2,18},{18,2},{3,19},{19,3},{4,20},{20... | collective-permute-start | bytes 3145736 | tf_op jit(solution)/shard_map/ppermute | solution.py:555
  396.6 88.1 %all-to-all-start.2 = ((bf16[4,128,1024]{2,1,0:T(8,128)(2,1)}), bf16[4,128,1024]{2,1,0:T(8,128)(2,1)S(1)}, u32[]{:S(2)}, u32[]{:S(2)}) async-start(bf16[4,128,1024]{2,1,0:T(8,128)(2,1)} %get-tuple-element.31), calls=%async_computation.2 | async-start | bytes 2097152 | tf_op jit(solution)/shard_map/all_to_all | solution.py:575
  405.1 49.8 %copy-start.4 = (f32[4,2,128,1024]{3,2,1,0:T(8,128)S(1)}, f32[4,2,128,1024]{3,2,1,0:T(8,128)}, u32[]{:S(2)}) copy-start(f32[4,2,128,1024]{3,2,1,0:T(8,128)} %get-tuple-element.47) | copy-start | bytes 12582916
  405.1 49.7 %collective-permute-start.9 = (bf16[256,768]{1,0:T(8,128)(2,1)S(1)}, bf16[256,768]{1,0:T(8,128)(2,1)S(1)}, u32[]{:S(2)}, u32[]{:S(2)}) collective-permute-start(bf16[256,768]{1,0:T(8,128)(2,1)S(1)} %dynamic-slice_convert_fusion.5), channel_id=1, source_target_pairs={{0,8},{4,12},{8,0},{12,4},{1,9},{5,13},{9,1},{13,5},{2,10},{6,14},... | collective-permute-start | bytes 1179656 | tf_op jit(solution)/shard_map/ppermute | solution.py:555
  408.0 69.3 %collective-permute-start.18 = (bf16[2,1024,128]{2,1,0:T(8,128)(2,1)S(1)}, bf16[2,1024,128]{2,1,0:T(8,128)(2,1)S(1)}, u32[]{:S(2)}, u32[]{:S(2)}) collective-permute-start(bf16[2,1024,128]{2,1,0:T(8,128)(2,1)S(1)} %dynamic-slice_convert_fusion.3), channel_id=1, source_target_pairs={{0,8},{4,12},{8,0},{12,4},{1,9},{5,13},{9,1},{13,5},{2,10},{6,14},... | collective-permute-start | bytes 1572872 | tf_op jit(solution)/shard_map/ppermute | solution.py:555
  458.4 23.1 %collective-permute-start.7 = (bf16[4,128,1024]{2,1,0:T(8,128)(2,1)S(1)}, bf16[4,128,1024]{2,1,0:T(8,128)(2,1)S(1)}, u32[]{:S(2)}, u32[]{:S(2)}) collective-permute-start(bf16[4,128,1024]{2,1,0:T(8,128)(2,1)S(1)} %fusion.19), channel_id=1, source_target_pairs={{0,2},{1,3},{2,0},{3,1},{4,6},{5,7},{6,4},{7,5},{8,10},{9,11},{10,... | collective-permute-start | bytes 3145736 | tf_op jit(solution)/shard_map/ppermute | solution.py:555
  459.1 10.2 %collective-permute-start.10 = (bf16[128,768]{1,0:T(8,128)(2,1)S(1)}, bf16[128,768]{1,0:T(8,128)(2,1)S(1)}, u32[]{:S(2)}, u32[]{:S(2)}) collective-permute-start(bf16[128,768]{1,0:T(8,128)(2,1)S(1)} %dynamic-slice_convert_fusion.9), channel_id=1, source_target_pairs={{0,4},{4,0},{8,12},{12,8},{1,5},{5,1},{9,13},{13,9},{2,6},{6,2},{1... | collective-permute-start | bytes 589832 | tf_op jit(solution)/shard_map/ppermute | solution.py:555
  460.7 20.8 %copy-start.3 = (bf16[4,128,1024]{2,1,0:T(8,128)(2,1)S(1)}, bf16[4,128,1024]{2,1,0:T(8,128)(2,1)}, u32[]{:S(2)}) copy-start(bf16[4,128,1024]{2,1,0:T(8,128)(2,1)} %copy-done.2) | copy-start | bytes 3145732
  460.7 20.8 %copy-start.21 = (f32[1024]{0:T(1024)S(1)}, f32[1024]{0:T(1024)}, u32[]{:S(2)}) copy-start(f32[1024]{0:T(1024)} %param.20) | copy-start | bytes 12292
  460.7 20.8 %copy-start.24 = (f32[4,128]{1,0:T(4,128)S(1)}, f32[4,128]{1,0:T(4,128)}, u32[]{:S(2)}) copy-start(f32[4,128]{1,0:T(4,128)} %copy-done.23) | copy-start | bytes 6148
  461.6 30.5 %collective-permute-start.15 = (bf16[2,128,1024]{2,1,0:T(8,128)(2,1)}, bf16[2,128,1024]{2,1,0:T(8,128)(2,1)}, u32[]{:S(2)}, u32[]{:S(2)}) collective-permute-start(bf16[2,128,1024]{2,1,0:T(8,128)(2,1)} %dynamic-slice_convert_fusion.4), channel_id=1, source_target_pairs={{0,8},{4,12},{8,0},{12,4},{1,9},{5,13},{9,1},{13,5},{2,10},{6,14},... | collective-permute-start | bytes 1572872 | tf_op jit(solution)/shard_map/ppermute | solution.py:555
  469.3 13.5 %copy-start.15 = (f32[4,128,1024]{2,1,0:T(8,128)S(1)}, f32[4,128,1024]{2,1,0:T(8,128)}, u32[]{:S(2)}) copy-start(f32[4,128,1024]{2,1,0:T(8,128)} %get-tuple-element.32) | copy-start | bytes 6291460
  484.7 73.4 %all-to-all-start.3 = ((bf16[4,128,1024]{2,1,0:T(8,128)(2,1)}), bf16[4,128,1024]{2,1,0:T(8,128)(2,1)}, u32[]{:S(2)}, u32[]{:S(2)}) async-start(bf16[4,128,1024]{2,1,0:T(8,128)(2,1)} %fusion.13), calls=%async_computation.3 | async-start | bytes 2097152 | tf_op jit(solution)/shard_map/all_to_all | solution.py:575
  488.9 24.4 %copy-start.12 = (f32[2,1024,128]{2,1,0:T(8,128)S(1)}, f32[2,1024,128]{2,1,0:T(8,128)}, u32[]{:S(2)}) copy-start(f32[2,1024,128]{2,1,0:T(8,128)} %convert_add_fusion.3) | copy-start | bytes 3145732
  490.1 27.7 %copy-start.19 = (f32[4,1024]{1,0:T(4,128)S(1)}, f32[4,1024]{1,0:T(4,128)}, u32[]{:S(2)}) copy-start(f32[4,1024]{1,0:T(4,128)} %slice.85) | copy-start | bytes 49156
  490.1 23.2 %collective-permute-start.19 = (bf16[1,1024,128]{2,1,0:T(8,128)(2,1)S(1)}, bf16[1,1024,128]{2,1,0:T(8,128)(2,1)S(1)}, u32[]{:S(2)}, u32[]{:S(2)}) collective-permute-start(bf16[1,1024,128]{2,1,0:T(8,128)(2,1)S(1)} %dynamic-slice_convert_fusion.6), channel_id=1, source_target_pairs={{0,4},{4,0},{8,12},{12,8},{1,5},{5,1},{9,13},{13,9},{2,6},{6,2},{1... | collective-permute-start | bytes 786440 | tf_op jit(solution)/shard_map/ppermute | solution.py:555
  493.4 23.5 %collective-permute-start.16 = (bf16[1,128,1024]{2,1,0:T(8,128)(2,1)S(1)}, bf16[1,128,1024]{2,1,0:T(8,128)(2,1)S(1)}, u32[]{:S(2)}, u32[]{:S(2)}) collective-permute-start(bf16[1,128,1024]{2,1,0:T(8,128)(2,1)S(1)} %dynamic-slice_convert_fusion.7), channel_id=1, source_target_pairs={{0,4},{4,0},{8,12},{12,8},{1,5},{5,1},{9,13},{13,9},{2,6},{6,2},{1... | collective-permute-start | bytes 786440 | tf_op jit(solution)/shard_map/ppermute | solution.py:555
  513.4 47.9 %copy-start.1 = (s32[1,4]{1,0:T(1,128)S(1)}, s32[1,4]{1,0:T(1,128)}, u32[]{:S(2)}) copy-start(s32[1,4]{1,0:T(1,128)} %param.19) | copy-start | bytes 52
  (14 other events, 47.0 us)
Sparse Core Ops, SparseCore 0:
  10.7 60.3 all-gather.3
  73.7 54.7 all-gather.5
  130.7 47.6 all-gather.7

commit v3 on v2

--- a/solution.py
+++ b/solution.py
@@ -891,6 +891,375 @@
     )(attended, w_output, w_up, w_down, own_tokens, *grads, vectors, bias_up)
 
 
+def back_kernel(
+    q_ref,
+    k_ref,
+    v_ref,
+    do_ref,
+    o_ref,
+    lse_ref,
+    key_bias_ref,
+    causal_ref,
+    w_ref,
+    tok_ref,
+    gmid_ref,
+    res_ref,
+    gdown_ref,
+    gup_ref,
+    gout_ref,
+    gain_ref,
+    sums_ref,
+    sum_up_ref,
+    normed_ref,
+    res_out,
+    gtok_out,
+    down_out,
+    up_out,
+    out_out,
+    proj_out,
+    shared_out,
+    by_col_out,
+    dk_sum,
+    dv_sum,
+    dproj,
+    gproj,
+    kept,
+    core_out,
+    core_in,
+    far_out,
+    far_in,
+    gtok,
+    norm_tile,
+    x_down,
+    x_up,
+    x_out,
+    x_proj,
+    z_down,
+    z_up,
+    z_out,
+    z_proj,
+    vec,
+    vec_in,
+    res_send,
+    res_recv,
+    tok_send,
+    tok_recv,
+    fold_send,
+    fold_recv,
+    x_send,
+    x_recv,
+    z_send,
+    z_recv,
+    vec_send,
+    vec_recv,
+    tile_sem,
+):
+    chunks, own, width = tok_ref.shape
+    rows = 4 * own
+    head_width = q_ref.shape[1]
+    core, far = peers()
+    row = lax.axis_index("row")
+    dp = lax.axis_index("dp")
+    cross = {"dp": 1 - dp}
+    other = lambda r: {"row": r}
+    sets = (
+        (gdown_ref, x_down, z_down, down_out),
+        (gup_ref, x_up, z_up, up_out),
+        (gout_ref, x_out, z_out, out_out),
+        (gproj, x_proj, z_proj, proj_out),
+    )
+
+    barrier = pltpu.get_barrier_semaphore()
+    for device in (core, far, cross, other((row + 1) % 4), other((row + 2) % 4), other((row + 3) % 4)):
+        pl.semaphore_signal(barrier, inc=1, device_id=device, device_id_type=pl.DeviceIdType.MESH)
+    pl.semaphore_wait(barrier, 6)
+
+    def trade(r, source, target, send, recv):
+        return remote(source.at[r], target.at[row], send.at[r], recv.at[row], other(r))
+
+    def trade_start(r, source, target, send, recv):
+        @pl.when(row != r)
+        def _():
+            trade(r, source, target, send, recv).start()
+
+        @pl.when(row == r)
+        def _():
+            target[r] = source[r]
+
+    def trade_wait(source, target, send, recv):
+        for r in range(4):
+
+            @pl.when(row != r)
+            def _():
+                trade(r, source, target, send, recv).wait_send()
+                remote(source.at[r], target.at[r], send.at[r], recv.at[r], other(r)).wait_recv()
+
+    def x_copy(i):
+        grads, arrived, _, _ = sets[i]
+        return remote(grads.at[pl.ds((1 - dp) * 4, 4)], arrived, x_send.at[i], x_recv.at[i], cross)
+
+    def x_add(i):
+        grads, arrived, _, _ = sets[i]
+        x_copy(i).wait()
+        for b in range(4):
+            arrived[b] = (arrived[b].astype(F32) + grads[dp * 4 + b].astype(F32)).astype(LOW)
+
+    def lanes(d):
+        place = row if d == 0 else 3 - row
+        following = {"row": jnp.minimum(row + 1, 3)} if d == 0 else {"row": jnp.maximum(row - 1, 0)}
+        return place, following
+
+    def z_first(i, d, k):
+        _, sums, moving, _ = sets[i]
+        place, following = lanes(d)
+        block = 3 - k if d == 0 else k
+        return remote(sums.at[block], moving.at[d, k], z_send.at[i, d, k], z_recv.at[i, d, k], following)
+
+    def z_next(i, d, k):
+        _, sums, moving, _ = sets[i]
+        place, following = lanes(d)
+        return remote(moving.at[d, k - 1], moving.at[d, k], z_send.at[i, d, k], z_recv.at[i, d, k], following)
+
+    def z_pump(i, k):
+        _, sums, moving, _ = sets[i]
+        for d in range(2):
+            place, following = lanes(d)
+
+            @pl.when(place == 0)
+            def _():
+                z_first(i, d, k).start()
+
+            if k >= 1:
+
+                @pl.when((place >= 1) & (place <= k))
+                def _():
+                    block = 3 - k + place if d == 0 else k - place
+                    z_first(i, d, k - 1).wait_recv()
+                    moving[d, k - 1] = (moving[d, k - 1].astype(F32) + sums[block].astype(F32)).astype(LOW)
+                    z_next(i, d, k).start()
+
+    def z_finish(i):
+        _, sums, moving, out = sets[i]
+        out[...] = sums[row].astype(F32)
+        for d in range(2):
+            place, following = lanes(d)
+
+            @pl.when(place >= 1)
+            def _():
+                z_first(i, d, 2).wait_recv()
+                out[...] += moving[d, 2].astype(F32)
+
+        for d in range(2):
+            place, following = lanes(d)
+            for k in range(3):
+
+                @pl.when(place <= k)
+                def _():
+                    z_first(i, d, k).wait_send()
+
+    for i in range(3):
+        x_copy(i).start()
+    for r in range(4):
+        trade_start(r, res_ref, res_out, res_send, res_recv)
+
+    block = 256
+    lane = lax.broadcasted_iota(jnp.int32, (block, 128), 1)
+
+    def attention(r):
+        wide = (r + 1) * rows
+
+        def part(step, carry):
+            here = pl.ds(pl.multiple_of(r * rows + (step % 2) * block, block), block)
+            pair = pl.ds(pl.multiple_of((step // 2) * 128, 128), 128)
+            inside = pl.ds(pl.multiple_of((step % 2) * block, block), block)
+            queries = q_ref[here, pair]
+            grads = do_ref[here, pair]
+            inner = (grads.astype(F32) * o_ref[here, pair].astype(F32)).T
+            parts = []
+            for head in range(2):
+                mine = (lane // HD) == head
+                masked = jnp.where(mine, queries, 0) * jnp.asarray(HD**-0.5, LOW)
+                masked_grads = jnp.where(mine, grads, 0)
+                inner_row = jnp.sum(inner[head * HD : (head + 1) * HD], axis=0, keepdims=True)
+                scores = contract(k_ref[:wide, pair], masked, 1, 1) + key_bias_ref[:wide]
+                last = scores[wide - rows :] + causal_ref[:, inside]
+                scores = last if r == 0 else jnp.concatenate([scores[: wide - rows], last], axis=0)
+                weights = jnp.exp(scores - lse_ref[step // 2, r, head : head + 1, inside])
+                grad_weights = contract(v_ref[:wide, pair], masked_grads, 1, 1)
+                grad_scores = (weights * (grad_weights - inner_row)).astype(LOW)
+                dv_sum[:wide, pair] += contract(weights.astype(LOW), masked_grads, 1, 0)
+                dk_sum[:wide, pair] += contract(grad_scores, masked, 1, 0)
+                parts.append(contract(grad_scores, k_ref[:wide, pair], 0, 0))
+            dproj[here, pair] = (jnp.where(lane < HD, parts[0], parts[1]) * HD**-0.5).astype(LOW)
+            return carry
+
+        lax.fori_loop(0, 4, part, 0)
+        end = slice(wide - rows, wide)
+        dproj[end, head_width : 2 * head_width] = dk_sum[end].astype(LOW)
+        dproj[end, 2 * head_width :] = dv_sum[end].astype(LOW)
+
+    def core_copy(r):
+        return remote(core_out.at[r], core_in.at[r], fold_send.at[0, r], fold_recv.at[0, r], core)
+
+    def far_copy(r):
+        return remote(far_out.at[r], far_in.at[r], fold_send.at[1, r], fold_recv.at[1, r], far)
+
+    def project(r):
+        total = contract(dproj[r * rows : (r + 1) * rows], w_ref[...], 1, 1)
+        kept[r, 0] = total[:own]
+        core_out[r, 0] = total[own : 2 * own].astype(LOW)
+        kept[r, 1] = total[2 * own : 3 * own]
+        core_out[r, 1] = total[3 * own :].astype(LOW)
+        core_copy(r).start()
+
+    def fold(r):
+        core_copy(r).wait()
+        far_out[r] = (kept[r, 1] + core_in[r, 1].astype(F32)).astype(LOW)
+        kept[r, 0] = kept[r, 0] + core_in[r, 0].astype(F32)
+        far_copy(r).start()
+
+    vec[...] = jnp.zeros_like(vec)
+
+    def norm_grad(r):
+        far_copy(r).wait()
+        grads = kept[r, 0] + far_in[r].astype(F32)
+        unit, scale = norm_parts(tok_ref[r].astype(F32))
+        gtok[r] = (gmid_ref[r] + norm_back(grads, gain_ref[...], unit, scale)).astype(LOW)
+        trade_start(r, gtok, gtok_out, tok_send, tok_recv)
+        vec[0:1] += jnp.sum(grads * unit, axis=0, keepdims=True)
+        vec[1:2] += jnp.sum(grads, axis=0, keepdims=True)
+
+    def tile_copy(t):
+        part = slice(t * 256, (t + 1) * 256)
+        return pltpu.make_async_copy(normed_ref.at[:, part], norm_tile.at[t % 2], tile_sem.at[t % 2])
+
+    dk_sum[...] = jnp.zeros_like(dk_sum)
+    dv_sum[...] = jnp.zeros_like(dv_sum)
+    tile_copy(0).start()
+    tile_copy(1).start()
+    attention(3)
+    project(3)
+    fold(3)
+    attention(2)
+    project(2)
+    fold(2)
+    x_add(0)
+    z_pump(0, 0)
+    attention(1)
+    project(1)
+    fold(1)
+    norm_grad(3)
+    z_pump(0, 1)
+    attention(0)
+    project(0)
+    fold(0)
+    for t in range(width // 256):
+        tile_copy(t).wait()
+        total = contract(norm_tile[t % 2], dproj[...], 0, 0).astype(LOW)
+        gproj[2 * t] = total[:own]
+        gproj[2 * t + 1] = total[own:]
+        if t + 2 < width // 256:
+            tile_copy(t + 2).start()
+    x_copy(3).start()
+    norm_grad(2)
+    z_pump(0, 2)
+    x_add(1)
+    z_pump(1, 0)
+    norm_grad(1)
+    z_pump(1, 1)
+    norm_grad(0)
+    x_add(2)
+    z_pump(2, 0)
+    z_pump(1, 2)
+    x_add(3)
+    z_pump(3, 0)
+    z_pump(2, 1)
+    z_pump(3, 1)
+    z_pump(2, 2)
+    z_pump(3, 2)
+
+    vec[2:6] = sums_ref[0:4]
+    vec[8:9] = sum_up_ref[...]
+    low_sum = jnp.sum(dproj[:, :head_width].astype(F32), axis=0, keepdims=True)
+    value_sum = jnp.sum(dproj[:, 2 * head_width :].astype(F32), axis=0, keepdims=True)
+    vec[9:10, :head_width] = low_sum
+    vec[9:10, head_width : 2 * head_width] = value_sum
+    steps = (cross, other(row + 1 - 2 * (row % 2)), other((row + 2) % 4), core, far)
+    for step, device in enumerate(steps):
+        size = 16 if step < 3 else 8
+        copy = remote(vec.at[:size], vec_in.at[step, :size], vec_send.at[step], vec_recv.at[step], device)
+        copy.start()
+        copy.wait()
+        vec[:size] = vec[:size] + vec_in[step, :size]
+    shared_out[...] = vec[:8]
+    by_col_out[...] = vec[8:]
+
+    for i in range(4):
+        z_finish(i)
+    trade_wait(res_ref, res_out, res_send, res_recv)
+    trade_wait(gtok, gtok_out, tok_send, tok_recv)
+
+
+def back_block(
+    queries, keys, values, grads, attended, lse, key_bias, causal, w_proj, tokens, gmid, result, gdown, gup, gout, gain, sums, sum_up, normed
+):
+    chunks, own, width = tokens.shape
+    rows, head_width = queries.shape
+    half = (chunks, 2, own, width)
+    one = (chunks, own, width)
+    blocks = ((gdown.shape[1], gdown.shape[2]), (gup.shape[1], gup.shape[2]), (gout.shape[1], gout.shape[2]), (own, 3 * head_width))
+    vmem = pl.BlockSpec(memory_space=pltpu.VMEM)
+    hbm = pl.BlockSpec(memory_space=pl.ANY)
+    dma = pltpu.SemaphoreType.DMA
+    return pl.pallas_call(
+        back_kernel,
+        in_specs=[vmem] * 18 + [hbm],
+        out_specs=[vmem] * 8,
+        out_shape=[jax.ShapeDtypeStruct(one, LOW), jax.ShapeDtypeStruct(one, LOW)]
+        + [jax.ShapeDtypeStruct(shape, F32) for shape in blocks]
+        + [jax.ShapeDtypeStruct((8, width), F32)] * 2,
+        scratch_shapes=[
+            pltpu.VMEM((rows, head_width), F32),
+            pltpu.VMEM((rows, head_width), F32),
+            pltpu.VMEM((rows, 3 * head_width), LOW),
+            pltpu.VMEM((8, own, 3 * head_width), LOW),
+            pltpu.VMEM(half, F32),
+            pltpu.VMEM(half, LOW),
+            pltpu.VMEM(half, LOW),
+            pltpu.VMEM(one, LOW),
+            pltpu.VMEM(one, LOW),
+            pltpu.VMEM(one, LOW),
+            pltpu.VMEM((2, rows, 256), LOW),
+        ]
+        + [pltpu.VMEM((4,) + shape, LOW) for shape in blocks]
+        + [pltpu.VMEM((2, 3) + shape, LOW) for shape in blocks]
+        + [
+            pltpu.VMEM((16, width), F32),
+            pltpu.VMEM((5, 16, width), F32),
+            dma((4,)),
+            dma((4,)),
+            dma((4,)),
+            dma((4,)),
+            dma((2, 4)),
+            dma((2, 4)),
+            dma((4,)),
+            dma((4,)),
+            dma((4, 2, 3)),
+            dma((4, 2, 3)),
+            dma((5,)),
+            dma((5,)),
+            dma((2,)),
+        ],
+        compiler_params=pltpu.CompilerParams(
+            collective_id=2, has_side_effects=True, vmem_limit_bytes=61 * 1024 * 1024
+        ),
+        cost_estimate=pl.CostEstimate(flops=100_000_000_000, bytes_accessed=30_000_000, transcendentals=0),
+        name="back_block",
+    )(
+        queries, keys, values, grads, attended, lse, key_bias, causal, w_proj, tokens, gmid, result, gdown, gup, gout, gain, sums, sum_up, normed
+    )
+
+
 def local_sequence(
     tokens,
     lengths,
@@ -960,40 +1329,26 @@
     result, grad_attended, grad_middle, grad_output, grad_up, grad_down, sums, sum_up = feed_block(
         attended, output_full, up_full, down_full, inputs_low, grad_all, vectors, bias_up.reshape(1, -1)
     )
-    result = trade_rows(result)
-    grad_queries, grad_keys, grad_values = attention_back(
-        queries, keys, values, grad_attended, attended, lse, key_bias, causal
-    )
-    grad_projected = jnp.concatenate([grad_queries, grad_keys, grad_values], axis=1)
-    grad_w = transposed_left(normed_all, grad_projected)
-    grad_first = scatter_rows(split_rows(transposed_right(grad_projected, query_key_value)))
-    first_unit, first_scale = norm_parts(inputs)
-    grad_tokens = grad_middle + norm_back(grad_first, first_gain, first_unit, first_scale)
-    grad_tokens = trade_rows(grad_tokens.astype(LOW))
-
-    grad_w = scatter_blocks(grad_w, 0)
-    grad_output = scatter_blocks(grad_output, 0)[0]
-    grad_down = scatter_blocks(grad_down, 0)[0]
-    grad_up = scatter_blocks(grad_up, 0)[0]
-
-    def over_rows(array):
-        return jnp.sum(array.astype(F32).reshape(-1, array.shape[-1]), axis=0)
-
-    shared = lax.psum(
-        jnp.stack(
-            [
-                over_rows(grad_first * first_unit),
-                over_rows(grad_first),
-                sums[0],
-                sums[1],
-                sums[2],
-                sums[3],
-            ]
-        ),
-        ("dp", "row", "col"),
-    )
-    by_col = lax.psum(
-        jnp.concatenate([over_rows(grad_queries), over_rows(grad_values), sum_up[0]]), ("dp", "row")
+    result, grad_tokens, grad_down, grad_up, grad_output, grad_w, shared, by_col = back_block(
+        queries,
+        keys,
+        values,
+        grad_attended,
+        attended,
+        lse,
+        key_bias.reshape(seq_rows, 1),
+        causal.T,
+        query_key_value,
+        inputs_low,
+        grad_middle,
+        result,
+        grad_down,
+        grad_up,
+        grad_output,
+        first_gain.reshape(1, width),
+        sums,
+        sum_up,
+        normed_all,
     )
     return (
         result,
@@ -1003,14 +1358,14 @@
         grad_w[:, :head_width],
         grad_w[:, head_width : 2 * head_width],
         grad_w[:, 2 * head_width :],
-        by_col[:head_width],
-        by_col[head_width : 2 * head_width],
+        by_col[1, :head_width],
+        by_col[1, head_width : 2 * head_width],
         grad_output,
         shared[2],
         shared[3],
         shared[4],
         grad_up,
-        by_col[2 * head_width :],
+        by_col[0],
         grad_down,
         shared[5],
     )

time: 575 us -> 465 us (0.81)
  Pallas kernels: 186 us -> 285 us
  waiting for transfers between devices: 155 us -> 62 us
  blocking collectives: 101 us -> 40.4 us
  starting transfers between devices: 29.5 us -> 8.16 us
  other arithmetic: 37.8 us -> 19.5 us
  local copies, waits for them, and re-layouts: 31.1 us -> 23.5 us
  matrix products: 12.6 us -> 5.67 us
    pallas_call x1, Pallas kernels: 34.7 us -> 133 us  [back_block(): pl.pallas_call(back_kernel, in_specs=[vmem] * 18 + [hbm], out_specs=[vmem...]
    ppermute x20 -> x6, waiting for transfers between devices: 110 us -> 14.5 us  [swap(): lax.ppermute(array, axis, [(place, place ^ flip) for place in range(size)])]
    psum x2 -> x0, blocking collectives: 60.2 us -> none  [the longest x1 39.6 us: local_sequence(): lax.psum(jnp.stack([over_rows(grad_first * first_unit), over_rows(grad_fi...]
    ppermute x20 -> x6, starting transfers between devices: 16.8 us -> 3.6 us  [swap(): lax.ppermute(array, axis, [(place, place ^ flip) for place in range(size)])]
    add x10 -> x0, other arithmetic: 10.6 us -> none  [the longest x9 7.27 us: scatter_blocks(): total = mine + swap(other.astype(LOW), axis, flip).astype(F32)]
    all_to_all x3 -> x1, starting transfers between devices: 12.6 us -> 4.48 us  [trade_rows(): return lax.all_to_all(array, 'row', split_axis=0, concat_axis=0)]
    dot_general x2 -> x0, matrix products: 6.97 us -> none  [the longest x1 3.51 us: transposed_left(): lax.dot_general(former, latter, (((0,), (0,)), ((), ())), preferred_eleme...]
    all_to_all x3 -> x1, waiting for transfers between devices: 29.2 us -> 29.4 us  [trade_rows(): return lax.all_to_all(array, 'row', split_axis=0, concat_axis=0)]
  transfers between devices with their start and end apart: 26 -> 10, of which waited for: 12 -> 3; matrix products, arithmetic and copies ran while one was open for 11% -> 7% of each run, Pallas kernels for 4% -> 5%
where the time goes in v3:
time: 465 us; the launch traced here: 459 us
  Pallas kernels  285 us (61%)
  waiting for transfers between devices  62 us (13%)
  blocking collectives  40.4 us (9%)
  local copies, waits for them, and re-layouts  23.5 us (5%)
  other arithmetic  19.5 us (4%)
  between operations  14.3 us (3%)
  starting transfers between devices  8.16 us (2%)
  matrix products  5.67 us (1%)
    pallas_call x1, Pallas kernels, back_block(): pl.pallas_call(back_kernel, in_specs=[vmem] * 18 + [hbm], out_specs=[vmem...  133 us
    pallas_call x1, Pallas kernels, feed_block(): pl.pallas_call(feed_kernel, in_specs=[vmem] * 5 + [hbm] * 4 + [vmem] * 2,...  127 us
    all_to_all x1, blocking collectives, trade_rows(): return lax.all_to_all(array, 'row', split_axis=0, concat_axis=0)  40.4 us
    all_to_all x1, waiting for transfers between devices, trade_rows(): return lax.all_to_all(array, 'row', split_axis=0, concat_axis=0)  29.4 us
    pallas_call x1, Pallas kernels, attention_out(): pl.pallas_call(attention_out_kernel, grid=(pairs, chunks), in_specs=[row_...  24.6 us
    all_gather x1, waiting for transfers between devices, local_sequence(): up_full = lax.all_gather(w_up, ('dp', 'row'), axis=0, tiled=True)  18 us
    ppermute x6, waiting for transfers between devices, swap(): lax.ppermute(array, axis, [(place, place ^ flip) for place in range(size)])  14.5 us
  transfers between devices with their start and end apart: 10, of which 3 were waited for; matrix products, arithmetic and copies ran while one was open for 7% of the time, Pallas kernels for 5%

profile of v3, /device:TPU:0, one launch (start us, length us, event | category | flops | bytes accessed | tf_op | source)
XLA Modules:
  0.0 458.9 jit_solution(10027675462056728589)
XLA Ops:
  7.2 0.0 copy-start
  7.2 0.0 all-gather.4.cloned.1.call-start
  7.3 1.6 pad_maximum_fusion.1
  8.8 0.0 all-gather.4.cloned.1.call-update
  8.9 0.0 copy-start.10
  8.9 0.0 copy-start.13
  8.9 0.0 all-gather.6.cloned.1.call-start
  9.0 1.7 pad_maximum_fusion
  10.7 0.0 all-gather.6.cloned.1.call-update
  10.7 40.4 %all_to_all.10.tok_ref = bf16[4,128,1024]{2,1,0:T(8,128)(2,1)S(1)} all-to-all(bf16[4,128,1024]{2,1,0:T(8,128)(2,1)} %param.18), channel_id=1, replica_groups=mesh['dp'=2,'row'=4,'col'=4] {'row'}, dimensions={0} | all-to-all | bytes 2097152 | tf_op jit(solution)/shard_map/all_to_all | solution.py:575
  51.1 4.5 all-to-all-start.1
  55.6 1.6 collective-permute-start.1
  57.2 0.1 iota_add_fusion
  57.2 0.6 constant_dynamic-slice_fusion
  57.8 0.7 convert_bitcast_fusion
  58.5 29.4 %all-to-all-done.1 = bf16[4,128,1024]{2,1,0:T(8,128)(2,1)} async-done(((bf16[4,128,1024]{2,1,0:T(8,128)(2,1)}), bf16[4,128,1024]{2,1,0:T(8,128)(2,1)}, u32[]{:S(2)}, u32[]{:S(2)}) %all-to-all-start.1) | async-done | bytes 1048608 | tf_op jit(solution)/shard_map/all_to_all | solution.py:575
  87.9 1.5 multiply_convert_fusion.g0_ref
  89.4 1.5 collective-permute-start.4
  90.9 0.5 collective-permute-start.2
  91.4 0.0 all-gather.8.cloned.1.call-update
  91.4 0.7 select_bitcast_fusion
  92.2 1.4 copy.45
  93.6 0.7 concatenate.11.vec_ref
  94.3 1.6 compare_select_fusion
  95.8 14.5 %collective-permute-done.4.g2_ref = bf16[4,128,1024]{2,1,0:T(8,128)(2,1)} collective-permute-done((bf16[4,128,1024]{2,1,0:T(8,128)(2,1)S(1)}, bf16[4,128,1024]{2,1,0:T(8,128)(2,1)}, u32[]{:S(2)}, u32[]{:S(2)}) %collective-permute-start.4) | collective-permute-done | bytes 1048608 | tf_op jit(solution)/shard_map/ppermute | solution.py:555
  110.4 1.9 fusion.7
  112.3 2.6 multiply_reduce_fusion
  114.9 1.9 maximum_convert_fusion
  116.9 1.7 copy.39
  118.6 3.4 fusion.3.normed_ref
  122.0 5.7 %fusion.11 = f32[2048,768]{1,0:T(8,128)S(1)} fusion(bf16[2048,1024]{1,0:T(8,128)(2,1)} %fusion.3.normed_ref, bf16[1024,768]{1,0:T(8,128)(2,1)} %all-gather.4.cloned.1.call-done.w_ref), kind=kOutput, calls=%fused_computation.32 | convolution fusion | flops 3221225472 | bytes 12058624 | tf_op jit(solution)/shard_map/dot_general | solution.py:28
  127.7 1.1 slice.86.k_ref
  128.7 1.8 fusion.4
  130.5 24.6 %attention_out.1 = (bf16[2048,256]{1,0:T(8,128)(2,1)}, f32[2,4,2,512]{3,2,1,0:T(2,128)}) custom-call(bf16[2048,256]{1,0:T(8,128)(2,1)} %get-tuple-element.54.q_ref, bf16[2048,256]{1,0:T(8,128)(2,1)} %slice.86.k_ref, bf16[2048,256]{1,0:T(8,128)(2,1)} %get-tuple-element.53.v_ref, f32[1,2048]{1,0:T(1,128)} %bitcast.54, f32[512,512]{1,0:T(8,128)} %get-tuple-element.67.causal_ref), custom_call_target="tpu_custom_call" | custom-call | flops 40000000000 | bytes 4000000 | tf_op jit(solution)/shard_map/attention_out/pallas_call | solution.py:460
  155.1 3.2 slice.77.wd_ref
  158.3 1.9 slice.76.wo_ref
  160.2 18.0 %all-gather.8.cloned.1.call-done.wu_ref = bf16[1024,1024]{1,0:T(8,128)(2,1)} async-done(((bf16[128,1024]{1,0:T(8,128)(2,1)}), bf16[1024,1024]{1,0:T(8,128)(2,1)}) %all-gather.8.cloned.1.call-update) | async-done | bytes 2097168 | tf_op jit(solution)/shard_map/all_gather | solution.py:1308
  178.2 127.3 %feed_block.1 = (bf16[4,128,1024]{2,1,0:T(8,128)(2,1)}, bf16[2048,256]{1,0:T(8,128)(2,1)}, f32[4,128,1024]{2,1,0:T(8,128)}, bf16[8,256,128]{2,1,0:T(8,128)(2,1)}...) custom-call(bf16[2048,256]{1,0:T(8,128)(2,1)} %get-tuple-element.35.att_, ...), custom_call_target="tpu_custom_call" | custom-call | flops 99999997952 | bytes 30000000 | tf_op jit(solution)/shard_map/feed_block/pallas_call | solution.py:850
  305.6 133.5 %back_block.1 = (bf16[4,128,1024]{2,1,0:T(8,128)(2,1)}, bf16[4,128,1024]{2,1,0:T(8,128)(2,1)}, f32[1024,128]{1,0:T(8,128)}, f32[128,1024]{1,0:T(8,128)}, f32[256...) custom-call(bf16[2048,256]{1,0:T(8,128)(2,1)} %get-tuple-element.54.q_ref, ...), custom_call_target="tpu_custom_call" | custom-call | flops 99999997952 | bytes 30000000 | tf_op jit(solution)/shard_map/back_block/pallas_call | solution.py:1214
  439.1 1.4 slice.71
  440.6 1.3 fusion.10
  441.9 1.8 fusion.8
  443.6 1.7 fusion.9
  445.3 2.3 copy.51
  447.6 2.3 copy.52
  449.9 0.7 copy.53
  450.5 0.8 copy.54
  451.3 0.8 copy.55
  (49 shorter events, 0.1 us)
Async XLA Ops:
  7.2 50.0 %copy-start = (s32[1,4]{1,0:T(1,128)S(1)}, s32[1,4]{1,0:T(1,128)}, u32[]{:S(2)}) copy-start(s32[1,4]{1,0:T(1,128)} %param.19) | copy-start | bytes 52
  7.2 114.8 %all-gather.4.cloned.1.call-start = ((), (), s32[]{:S(2)}) async-start(), calls=%async_computation.2 | async-start | bytes 1769472 | tf_op jit(solution)/shard_map/all_gather | solution.py:1303
  8.9 84.7 %copy-start.10 = (f32[1024]{0:T(1024)S(1)}, f32[1024]{0:T(1024)}, u32[]{:S(2)}) copy-start(f32[1024]{0:T(1024)} %param.28) | copy-start | bytes 12292
  8.9 84.7 %copy-start.11 = (f32[1024]{0:T(1024)S(1)}, f32[1024]{0:T(1024)}, u32[]{:S(2)}) copy-start(f32[1024]{0:T(1024)} %param.29) | copy-start | bytes 12292
  8.9 84.7 %copy-start.12 = (f32[1024]{0:T(1024)S(1)}, f32[1024]{0:T(1024)}, u32[]{:S(2)}) copy-start(f32[1024]{0:T(1024)} %param.30) | copy-start | bytes 12292
  8.9 84.7 %copy-start.13 = (f32[1024]{0:T(1024)S(1)}, f32[1024]{0:T(1024)}, u32[]{:S(2)}) copy-start(f32[1024]{0:T(1024)} %param.34) | copy-start | bytes 12292
  8.9 146.2 %all-gather.6.cloned.1.call-start = ((), (), s32[]{:S(2)}) async-start(), calls=%async_computation.3 | async-start | bytes 2949120 | tf_op jit(solution)/shard_map/all_gather | solution.py:1306
  51.1 63.8 %copy-start.2 = (bf16[4,128,1024]{2,1,0:T(8,128)(2,1)}, bf16[4,128,1024]{2,1,0:T(8,128)(2,1)S(1)}, u32[]{:S(2)}) copy-start(bf16[4,128,1024]{2,1,0:T(8,128)(2,1)S(1)} %all_to_all.10.tok_ref) | copy-start | bytes 3145732
  51.1 36.8 %all-to-all-start.1 = ((bf16[4,128,1024]{2,1,0:T(8,128)(2,1)}), bf16[4,128,1024]{2,1,0:T(8,128)(2,1)}, u32[]{:S(2)}, u32[]{:S(2)}) async-start(bf16[4,128,1024]{2,1,0:T(8,128)(2,1)} %param.35), calls=%async_computation.1 | async-start | bytes 2097152 | tf_op jit(solution)/shard_map/all_to_all | solution.py:575
  55.6 122.7 %all-gather.8.cloned.1.call-start = ((), (), s32[]{:S(2)}) async-start(), calls=%async_computation.4 | async-start | bytes 2359296 | tf_op jit(solution)/shard_map/all_gather | solution.py:1308
  55.6 35.3 %collective-permute-start.1 = (bf16[4,128,1024]{2,1,0:T(8,128)(2,1)S(1)}, bf16[4,128,1024]{2,1,0:T(8,128)(2,1)S(1)}, u32[]{:S(2)}, u32[]{:S(2)}) collective-permute-start(bf16[4,128,1024]{2,1,0:T(8,128)(2,1)S(1)} %all_to_all.10.tok_ref), channel_id=1, source_target_pairs={{0,2},{1,3},{2,0},{3,1},{4,6},{5,7},{6,4},{7,5},{8,10},{9,11},{10,... | collective-permute-start | bytes 3145736 | tf_op jit(solution)/shard_map/ppermute | solution.py:555
  89.4 25.5 %copy-start.3 = (bf16[4,128,1024]{2,1,0:T(8,128)(2,1)}, bf16[4,128,1024]{2,1,0:T(8,128)(2,1)S(1)}, u32[]{:S(2)}) copy-start(bf16[4,128,1024]{2,1,0:T(8,128)(2,1)S(1)} %multiply_convert_fusion.g0_ref) | copy-start | bytes 3145732
  89.4 21.0 %collective-permute-start.4 = (bf16[4,128,1024]{2,1,0:T(8,128)(2,1)S(1)}, bf16[4,128,1024]{2,1,0:T(8,128)(2,1)}, u32[]{:S(2)}, u32[]{:S(2)}) collective-permute-start(bf16[4,128,1024]{2,1,0:T(8,128)(2,1)S(1)} %multiply_convert_fusion.g0_ref), channel_id=1, source_target_pairs={{0,2},{1,3},{2,0},{3,1},{4,6},{5,7},{6,4},{7,5},{8,10},{9,11},{10,... | collective-permute-start | bytes 3145736 | tf_op jit(solution)/shard_map/ppermute | solution.py:555
  90.9 19.4 %collective-permute-start = (bf16[4,128,1024]{2,1,0:T(8,128)(2,1)S(1)}, bf16[4,128,1024]{2,1,0:T(8,128)(2,1)}, u32[]{:S(2)}, u32[]{:S(2)}) collective-permute-start(bf16[4,128,1024]{2,1,0:T(8,128)(2,1)S(1)} %all_to_all.10.tok_ref), channel_id=1, source_target_pairs={{0,1},{1,0},{2,3},{3,2},{4,5},{5,4},{6,7},{7,6},{8,9},{9,8},{10,11... | collective-permute-start | bytes 3145736 | tf_op jit(solution)/shard_map/ppermute | solution.py:555
  90.9 19.4 %collective-permute-start.2 = (bf16[4,128,1024]{2,1,0:T(8,128)(2,1)S(1)}, bf16[4,128,1024]{2,1,0:T(8,128)(2,1)}, u32[]{:S(2)}, u32[]{:S(2)}) collective-permute-start(bf16[4,128,1024]{2,1,0:T(8,128)(2,1)S(1)} %collective-permute-done.1), channel_id=1, source_target_pairs={{0,1},{1,0},{2,3},{3,2},{4,5},{5,4},{6,7},{7,6},{8,9},{9,8},{10,11... | collective-permute-start | bytes 3145736 | tf_op jit(solution)/shard_map/ppermute | solution.py:555
  92.2 22.7 %copy-start.7 = (f32[1,1,4,512]{3,1,2,0:T(1,128)}, f32[1,1,4,512]{3,1,2,0:T(1,128)S(1)}, u32[]{:S(2)}) copy-start(f32[1,1,4,512]{3,1,2,0:T(1,128)S(1)} %copy.43) | copy-start | bytes 24580
  95.8 64.3 %collective-permute-start.3 = (bf16[4,128,1024]{2,1,0:T(8,128)(2,1)S(1)}, bf16[4,128,1024]{2,1,0:T(8,128)(2,1)}, u32[]{:S(2)}, u32[]{:S(2)}) collective-permute-start(bf16[4,128,1024]{2,1,0:T(8,128)(2,1)S(1)} %multiply_convert_fusion.g0_ref), channel_id=1, source_target_pairs={{0,1},{1,0},{2,3},{3,2},{4,5},{5,4},{6,7},{7,6},{8,9},{9,8},{10,11... | collective-permute-start | bytes 3145736 | tf_op jit(solution)/shard_map/ppermute | solution.py:555
  110.3 49.9 %collective-permute-start.5 = (bf16[4,128,1024]{2,1,0:T(8,128)(2,1)}, bf16[4,128,1024]{2,1,0:T(8,128)(2,1)}, u32[]{:S(2)}, u32[]{:S(2)}) collective-permute-start(bf16[4,128,1024]{2,1,0:T(8,128)(2,1)} %collective-permute-done.4.g2_ref), channel_id=1, source_target_pairs={{0,1},{1,0},{2,3},{3,2},{4,5},{5,4},{6,7},{7,6},{8,9},{9,8},{10,11... | collective-permute-start | bytes 3145736 | tf_op jit(solution)/shard_map/ppermute | solution.py:555
  116.9 1.7 copy-start.8
  116.9 1.7 copy-start.9
  122.0 6.8 %copy-start.14 = (f32[256]{0:T(256)S(1)}, f32[256]{0:T(256)}, u32[]{:S(2)}) copy-start(f32[256]{0:T(256)} %param.26) | copy-start | bytes 3076
  122.0 6.8 %copy-start.15 = (f32[256]{0:T(256)S(1)}, f32[256]{0:T(256)}, u32[]{:S(2)}) copy-start(f32[256]{0:T(256)} %param.25) | copy-start | bytes 3076
  305.6 146.5 %copy-start.1 = (s32[1,4]{1,0:T(1,128)S(1)}, s32[1,4]{1,0:T(1,128)}, u32[]{:S(2)}) copy-start(s32[1,4]{1,0:T(1,128)} %param.19) | copy-start | bytes 52
  439.1 10.8 %copy-start.6 = (f32[256,128]{1,0:T(8,128)S(1)}, f32[256,128]{1,0:T(8,128)}, u32[]{:S(2)}) copy-start(f32[256,128]{1,0:T(8,128)} %get-tuple-element.96) | copy-start | bytes 393220
  439.1 11.4 %copy-start.5 = (f32[128,1024]{1,0:T(8,128)S(1)}, f32[128,1024]{1,0:T(8,128)}, u32[]{:S(2)}) copy-start(f32[128,1024]{1,0:T(8,128)} %get-tuple-element.100) | copy-start | bytes 1572868
  439.1 12.2 %copy-start.4 = (f32[1024,128]{1,0:T(8,128)S(1)}, f32[1024,128]{1,0:T(8,128)}, u32[]{:S(2)}) copy-start(f32[1024,128]{1,0:T(8,128)} %get-tuple-element.102) | copy-start | bytes 1572868
Sparse Core Ops, SparseCore 0:
  10.7 60.4 all-gather.3
  73.8 54.7 all-gather.5
  130.7 47.4 all-gather.7
